TPU v7x, 768 devices: a whole 4x8x12 slice. The times are simulated.
768 devices in a mesh: dp: 32 (over x, y), ctx: 24 (over z, core).
Axes of the slice: x: 4, y: 8, z: 12, core: 2. Of those that a mesh axis runs over, the one named last changes fastest.
Arguments:
- tokens: bfloat16 [6144, 5120], P('dp'), may hold values from -6 to 6
- scores: float32 [6144, 8], P('dp'), may hold values from -12 to 12
- routes: int32 [6144, 1], P('dp'), may hold values from 0 to 127; in each aligned block of 192 rows (0 to 191, 192 to 383, ...) at most 4 rows name the same one
- w_gate: bfloat16 [5120, 98304], P(None, ('dp', 'ctx')), may hold values from -0.078125 to 0.078125
- w_up: bfloat16 [5120, 98304], P(None, ('dp', 'ctx')), may hold values from -0.078125 to 0.078125
- w_down: bfloat16 [98304, 5120], P(('dp', 'ctx')), may hold values from -0.21875 to 0.21875
Outputs:
- mixed: bfloat16 [6144, 5120], P(('dp', 'ctx'))
Inputs may be any that keep to these rules, and one draw needn't show every extreme that they name: Within each aligned block of 192 tokens (the tokens of one index of dp), a token's 1 routes name different experts, no expert is named more than 4 times in the block, a bound that some block reaches.
All inputs are finite; a program needn't handle non-finite values.
Results may differ from a plain program's by a relative error of at most 0.006.
Values may be sent and summed in bfloat16 or wider, within the bound.
No kernel may reach another device: no remote copies, remote signals or barrier semaphores. Data moves between devices by JAX's collectives and lax.ppermute only.
A program may use at most 32 MiB of HBM per device.

v0:
```python
import jax
import jax.numpy as jnp
from jax import lax
from jax.sharding import PartitionSpec as P

EXP_DP = 4
CAP = 4


route_scale = 2.5


def per_device(tokens, scores, routes, w_gate, w_up, w_down):
    dp_count = lax.axis_size("dp")
    ctx_count = lax.axis_size("ctx")
    parts = ctx_count // EXP_DP
    my_group = lax.axis_index("ctx") // parts
    tok_rows = tokens.shape[0]
    model_width = tokens.shape[1]
    flying = routes.shape[1]
    per_block = tok_rows * flying
    sig = jax.nn.sigmoid(scores)
    gates = route_scale * sig[:, :flying] / jnp.sum(sig, axis=1, keepdims=True)
    flat_routes = routes.reshape(-1)
    onehot = (
        flat_routes[:, None] == jnp.arange(EXP_DP * dp_count, dtype=jnp.int32)[None, :]
    ).astype(jnp.int32)
    before = jnp.cumsum(onehot, axis=0) - onehot
    slot = jnp.sum(before * onehot, axis=1)
    target_dp = flat_routes // EXP_DP
    mine = flat_routes % EXP_DP == my_group
    position = jnp.where(mine, target_dp * CAP + slot, dp_count * CAP)
    table = jnp.full((dp_count * CAP,), per_block, jnp.int32)
    table = table.at[position].set(jnp.arange(per_block, dtype=jnp.int32), mode="drop")
    token_of = table // flying
    padded = jnp.concatenate([tokens, jnp.zeros((1, model_width), tokens.dtype)], axis=0)
    outgoing = padded[token_of].reshape(dp_count, CAP, model_width)
    arrived = lax.all_to_all(outgoing, "dp", split_axis=0, concat_axis=0, tiled=True)
    rows = arrived.reshape(-1, model_width)
    pre_gate = jnp.dot(rows, w_gate, preferred_element_type=jnp.float32)
    pre_up = jnp.dot(rows, w_up, preferred_element_type=jnp.float32)
    hidden = (jax.nn.silu(pre_gate) * pre_up).astype(jnp.bfloat16)
    piece = jnp.dot(hidden, w_down, preferred_element_type=jnp.float32).astype(jnp.bfloat16)
    returned = lax.all_to_all(
        piece.reshape(arrived.shape), "dp", split_axis=0, concat_axis=0, tiled=True
    )
    flat_gates = jnp.concatenate([gates.reshape(-1), jnp.zeros((1,), jnp.float32)])
    slot_weights = flat_gates[table]
    weighted = returned.reshape(-1, model_width).astype(jnp.float32) * slot_weights[:, None]
    term = jnp.zeros((tok_rows + 1, model_width), jnp.float32).at[token_of].add(weighted)[:tok_rows]
    summed = lax.psum_scatter(term, "ctx", scatter_dimension=0, tiled=True)
    return summed.astype(jnp.bfloat16)


def solution(mesh):
    in_specs = (
        P("dp", None),
        P("dp", None),
        P("dp", None),
        P(None, ("dp", "ctx")),
        P(None, ("dp", "ctx")),
        P(("dp", "ctx"), None),
    )
    out_specs = P(("dp", "ctx"), None)
    return jax.shard_map(
        per_device, mesh=mesh, in_specs=in_specs, out_specs=out_specs, check_vma=False
    )
```

profile of v0, /device:TPU:6, one launch (start us, length us, event | category | flops | bytes accessed | tf_op | source)
XLA Modules:
  0.0 227.0 jit_solution(18191481926312597351)
XLA Ops:
  6.5 0.0 copy-start
  6.5 0.9 iota_compare_fusion
  7.4 0.1 fusion.5
  7.7 0.9 fusion.8
  8.6 0.7 compare_select_fusion
  9.3 1.2 scatter_custom_fusion
  10.5 1.8 concatenate.6
  12.3 2.4 %gather_fusion = bf16[128,5120]{1,0:T(8,128)(2,1)} fusion(bf16[193,5120]{1,0:T(8,128)(2,1)S(1)} %concatenate.6, s32[1024]{0:T(1024)S(1)} %pad_clamp_fusion), kind=kCustom, calls=%fused_computation | custom fusion | bytes 2621952 | tf_op jit(solution)/shard_map/gather | solution.py:37
  14.6 2.6 %reshape.31 = bf16[32,4,5120]{2,1,0:T(4,128)(2,1)S(1)} reshape(bf16[128,5120]{1,0:T(8,128)(2,1)} %gather_fusion) | data formatting | bytes 2621440 | tf_op jit(solution)/shard_map/reshape | solution.py:37
  17.2 43.1 %all_to_all.10 = bf16[32,4,5120]{2,1,0:T(4,128)(2,1)} all-to-all(bf16[32,4,5120]{2,1,0:T(4,128)(2,1)S(1)} %reshape.31), channel_id=1, replica_groups=mesh['dp'=32,'ctx'=24] {'dp'}, dimensions={0} | all-to-all | bytes 2621440 | tf_op jit(solution)/shard_map/all_to_all | solution.py:38
  60.3 2.5 %reshape.32 = bf16[128,5120]{1,0:T(8,128)(2,1)S(1)} reshape(bf16[32,4,5120]{2,1,0:T(4,128)(2,1)} %all_to_all.10) | data formatting | bytes 2621440 | tf_op jit(solution)/shard_map/reshape | solution.py:39
  62.8 1.8 fusion.20
  64.6 0.0 copy-done
  64.6 3.3 %convolution_convert_fusion = bf16[128,5120]{1,0:T(8,128)(2,1)} fusion(bf16[128,5120]{1,0:T(8,128)(2,1)S(1)} %copy-done, bf16[128,5120]{1,0:T(8,128)(2,1)S(1)} %reshape.32, bf16[5120,128]{1,0:T(8,128)(2,1)} %param.10, f32[128,128]{1,0:T(8,128)S(1)} %fusion.20), kind=kOutput, calls=%fused_computation.4 | convolution fusion | flops 336297984 | bytes 5308416 | tf_op jit(solution)/shard_map/dot_general | solution.py:43
  67.9 3.4 %reshape.33 = bf16[32,4,5120]{2,1,0:T(4,128)(2,1)} reshape(bf16[128,5120]{1,0:T(8,128)(2,1)} %convolution_convert_fusion) | data formatting | bytes 2621440 | tf_op jit(solution)/shard_map/reshape | solution.py:45
  71.3 0.0 copy-start.1
  71.4 6.5 %all-to-all-start.1 = ((bf16[32,4,5120]{2,1,0:T(4,128)(2,1)}), bf16[32,4,5120]{2,1,0:T(4,128)(2,1)S(1)}, u32[]{:S(2)}, u32[]{:S(2)}) async-start(bf16[32,4,5120]{2,1,0:T(4,128)(2,1)} %reshape.33), calls=%async_computation.1 | async-start | bytes 2621440 | tf_op jit(solution)/shard_map/all_to_all | solution.py:44
  77.8 0.0 reduce-scatter.2.cloned.1.call-start
  77.9 0.0 copy-done.1
  77.9 0.1 pad_maximum_fusion
  78.0 1.3 gather_fusion.1
  79.3 27.1 %all-to-all-done.1 = bf16[32,4,5120]{2,1,0:T(4,128)(2,1)S(1)} async-done(((bf16[32,4,5120]{2,1,0:T(4,128)(2,1)}), bf16[32,4,5120]{2,1,0:T(4,128)(2,1)S(1)}, u32[]{:S(2)}, u32[]{:S(2)}) %all-to-all-start.1) | async-done | bytes 1310752 | tf_op jit(solution)/shard_map/all_to_all | solution.py:44
  106.4 1.6 reshape.36
  108.0 7.3 %scatter_custom_fusion.1 = f32[193,5120]{1,0:T(8,128)} fusion(s32[128]{0:T(128)S(1)} %compare_select_fusion.2, f32[128,5120]{1,0:T(8,128)} %reshape.36, f32[]{:T(128)} %constant.63.clone.1, f32[128]{0:T(128)S(1)} %gather_fusion.1), kind=kCustom, calls=%fused_computation.5 | custom fusion | flops 1310720 | bytes 6574596 | tf_op jit(solution)/shard_map/scatter-add | solution.py:50
  115.3 4.4 %slice.27 = f32[192,5120]{1,0:T(8,128)} slice(f32[193,5120]{1,0:T(8,128)} %scatter_custom_fusion.1), slice={[0:192], [0:5120]} | slice | bytes 7864320 | tf_op jit(solution)/shard_map/slice | solution.py:50
  119.6 0.0 reduce-scatter.2.cloned.1.call-update
  119.7 98.9 %reduce-scatter.2.cloned.1.call-done = f32[8,5120]{1,0:T(8,128)} async-done(((f32[192,5120]{1,0:T(8,128)}), f32[8,5120]{1,0:T(8,128)}) %reduce-scatter.2.cloned.1.call-update) | async-done | bytes 163856 | tf_op jit(solution)/shard_map/reduce_scatter | solution.py:51
  218.6 1.6 convert_element_type.24
  (12 shorter events, 0.1 us)
Async XLA Ops:
  6.5 58.1 %copy-start = (bf16[128,5120]{1,0:T(8,128)(2,1)S(1)}, bf16[128,5120]{1,0:T(8,128)(2,1)}, u32[]{:S(2)}) copy-start(bf16[128,5120]{1,0:T(8,128)(2,1)} %param.11) | copy-start | bytes 3932164
  71.3 6.5 %copy-start.1 = (f32[192,8]{0,1:T(8,128)S(1)}, f32[192,8]{0,1:T(8,128)}, u32[]{:S(2)}) copy-start(f32[192,8]{0,1:T(8,128)} %param.7) | copy-start | bytes 18436
  71.4 35.0 %all-to-all-start.1 = ((bf16[32,4,5120]{2,1,0:T(4,128)(2,1)}), bf16[32,4,5120]{2,1,0:T(4,128)(2,1)S(1)}, u32[]{:S(2)}, u32[]{:S(2)}) async-start(bf16[32,4,5120]{2,1,0:T(4,128)(2,1)} %reshape.33), calls=%async_computation.1 | async-start | bytes 2621440 | tf_op jit(solution)/shard_map/all_to_all | solution.py:44
  77.8 140.8 %reduce-scatter.2.cloned.1.call-start = ((), (), s32[]{:S(2)}) async-start(), calls=%async_computation.3 | async-start | bytes 4096000 | tf_op jit(solution)/shard_map/reduce_scatter | solution.py:51
Sparse Core Ops, SparseCore 0:
  119.8 98.7 reduce-scatter.1
where the time goes:
time: 228 us; the launch traced here: 227 us
  waiting for transfers between devices  126 us (55%)
  blocking collectives  43.1 us (19%)
  local copies, waits for them, and re-layouts  21 us (9%)
  between operations  13.6 us (6%)
  other arithmetic  11.6 us (5%)
  starting transfers between devices  6.51 us (3%)
  matrix products  5.13 us (2%)
    reduce_scatter x1, waiting for transfers between devices, per_device(): summed = lax.psum_scatter(term, 'ctx', scatter_dimension=0, tiled=True)  98.9 us
    all_to_all x1, blocking collectives, per_device(): lax.all_to_all(outgoing, 'dp', split_axis=0, concat_axis=0, tiled=True)  43.1 us
    all_to_all x1, waiting for transfers between devices, per_device(): lax.all_to_all(piece.reshape(arrived.shape), 'dp', split_axis=0, concat_a...  27.1 us
    scatter-add x1, other arithmetic, per_device(): jnp.zeros((tok_rows + 1, model_width), jnp.float32).at[token_of]  7.32 us
    all_to_all x1, starting transfers between devices, per_device(): lax.all_to_all(piece.reshape(arrived.shape), 'dp', split_axis=0, concat_a...  6.47 us
  transfers between devices with their start and end apart: 2, of which 2 were waited for; matrix products, arithmetic and copies ran while one was open for 1% of the time, Pallas kernels for 0%

commit v1 on v0

v1 whole, which is shorter than its diff:
```python
import functools

import jax
import jax.numpy as jnp
from jax import lax
from jax.experimental import pallas as pl
from jax.experimental.pallas import tpu as pltpu
from jax.sharding import Mesh
from jax.sharding import PartitionSpec as P

EXP_DP = 4
CAP = 4
CORES = 2
LANES = 128
ROUTE_SCALE = 2.5
VMEM_LIMIT = 48 * 1024 * 1024

VMEM = pl.BlockSpec(memory_space=pltpu.VMEM)
SMEM = pl.BlockSpec(memory_space=pltpu.SMEM)
PARAMS = pltpu.CompilerParams(vmem_limit_bytes=VMEM_LIMIT)


def slot_of_tokens(routes, group):
    tokens = routes.shape[0]
    row = lax.broadcasted_iota(jnp.int32, (tokens, tokens), 0)
    col = lax.broadcasted_iota(jnp.int32, (tokens, tokens), 1)
    across = jnp.broadcast_to(routes, (tokens, tokens))
    flat = jnp.sum(jnp.where(row == col, across, 0), axis=0, keepdims=True)
    same = (across == flat) & (row < col)
    rank = jnp.sum(same.astype(jnp.int32), axis=0, keepdims=True)
    slot = (flat >> 2) * CAP + rank
    return jnp.where((flat & 3) == group, slot, jnp.int32(1 << 20))


def pick_kernel(place_ref, routes_ref, tokens_ref, out_ref):
    slots, width = out_ref.shape
    tokens = routes_ref.shape[0]
    slot = slot_of_tokens(routes_ref[...], place_ref[0])
    rows = lax.broadcasted_iota(jnp.int32, (slots, tokens), 0)
    pick = jnp.where(rows == slot, 1.0, 0.0).astype(jnp.bfloat16)
    start = pl.multiple_of(place_ref[2] * width, LANES)
    out_ref[...] = jnp.dot(
        pick, tokens_ref[:, pl.ds(start, width)], preferred_element_type=jnp.float32
    ).astype(jnp.bfloat16)


def hidden_kernel(place_ref, own_ref, other_ref, gate_ref, up_ref, out_ref):
    half = own_ref.shape[1]
    mine = pl.multiple_of(place_ref[2] * half, LANES)
    theirs = pl.multiple_of((1 - place_ref[2]) * half, LANES)

    def project(w_ref):
        return jnp.dot(
            own_ref[...], w_ref[pl.ds(mine, half), :], preferred_element_type=jnp.float32
        ) + jnp.dot(
            other_ref[...], w_ref[pl.ds(theirs, half), :], preferred_element_type=jnp.float32
        )

    pre_gate = project(gate_ref)
    pre_up = project(up_ref)
    out_ref[...] = (pre_gate * jax.nn.sigmoid(pre_gate) * pre_up).astype(jnp.bfloat16)


def down_kernel(place_ref, hidden_ref, own_ref, next_ref, last_ref, swap_ref, out_ref):
    rows, width = out_ref.shape
    third = place_ref[1]
    core = place_ref[2]
    base = jnp.minimum(third * (2 * width), own_ref.shape[1] - 2 * width)
    here = pl.multiple_of(base + core * width, LANES)
    local = pl.multiple_of(core * width, LANES)
    total = jnp.zeros((rows, width), jnp.float32)
    for step in range(3):
        source = lax.rem(third + 3 - step, 3)
        if step == 0:
            weights = own_ref[:, pl.ds(here, width)]
        else:
            weights = (next_ref, last_ref)[step - 1][:, pl.ds(local, width)]
        total += jnp.dot(
            hidden_ref[2 * source + core], weights, preferred_element_type=jnp.float32
        )
        total += jnp.dot(
            hidden_ref[2 * source + 1 - core],
            swap_ref[step],
            preferred_element_type=jnp.float32,
        )
    out_ref[...] = total.astype(jnp.bfloat16)


def spread_kernel(place_ref, routes_ref, back_ref, out_ref):
    slots = back_ref.shape[0]
    tokens = out_ref.shape[0]
    slot = slot_of_tokens(routes_ref[...], place_ref[0])
    rows = lax.broadcasted_iota(jnp.int32, (slots, tokens), 0)
    pick = jnp.where(rows == slot, 1.0, 0.0).astype(jnp.bfloat16)
    out_ref[...] = lax.dot_general(
        pick, back_ref[...], (((0,), (0,)), ((), ())), preferred_element_type=jnp.float32
    ).astype(jnp.bfloat16)


def finish_kernel(place_ref, scores_ref, parts_ref, out_ref):
    rows, model = out_ref.shape
    width = parts_ref.shape[1]
    start = pl.multiple_of(place_ref[3] * rows, rows)
    sig = jax.nn.sigmoid(scores_ref[pl.ds(start, rows), :])
    gates = ROUTE_SCALE * sig[:, :1] / jnp.sum(sig, axis=1, keepdims=True)
    parts = parts_ref[...].astype(jnp.float32)
    per_group = parts.shape[0] // EXP_DP
    total = parts[:per_group]
    for group in range(1, EXP_DP):
        total = total + parts[group * per_group : (group + 1) * per_group]
    count = per_group // rows
    for part in range(count):
        third, core = part // CORES, part % CORES
        base = min(third * CORES * width, model - CORES * width) + core * width
        skip = max(0, third * CORES * width + core * width - base) if core == 0 else 0
        block = total[part * rows : (part + 1) * rows]
        out_ref[:, base + skip : base + width] = (block[:, skip:] * gates).astype(jnp.bfloat16)


def per_device(tokens, scores, routes, w_gate, w_up, w_down):
    dp_count = lax.axis_size("dp")
    model = tokens.shape[1]
    tok_rows = tokens.shape[0]
    hidden_units = w_down.shape[0]
    thirds = lax.axis_size("j")
    parts = thirds * CORES
    owners = EXP_DP * parts
    slots = dp_count * CAP
    half = model // CORES
    width = -(-model // (parts * LANES)) * LANES
    group, third, core = lax.axis_index("g"), lax.axis_index("j"), lax.axis_index("k")
    owner = (group * thirds + third) * CORES + core
    place = jnp.stack([group, third, core, owner]).astype(jnp.int32)
    bf = jnp.bfloat16

    def columns(to):
        start = jnp.minimum(to * (CORES * width), model - CORES * width)
        return lax.dynamic_slice_in_dim(w_down, start, CORES * width, 1)

    moved = []
    for step in (1, 2):
        moved.append(
            lax.ppermute(
                columns(lax.rem(third + step, thirds)),
                "j",
                [(i, (i + step) % thirds) for i in range(thirds)],
            )
        )
    mine_down = columns(third)
    away = (1 - core) * width
    swap = jnp.stack(
        [lax.dynamic_slice_in_dim(w, away, width, 1) for w in (mine_down, moved[0], moved[1])]
    )
    swapped = lax.ppermute(swap, "k", [(0, 1), (1, 0)])

    outgoing = pl.pallas_call(
        pick_kernel,
        out_shape=jax.ShapeDtypeStruct((slots, half), bf),
        in_specs=[SMEM, VMEM, VMEM],
        out_specs=VMEM,
        compiler_params=PARAMS,
    )(place, routes, tokens)
    arrived = lax.all_to_all(
        outgoing.reshape(dp_count, CAP, half), "dp", split_axis=0, concat_axis=0, tiled=True
    )
    other = lax.ppermute(arrived, "k", [(0, 1), (1, 0)])
    hidden = pl.pallas_call(
        hidden_kernel,
        out_shape=jax.ShapeDtypeStruct((slots, hidden_units), bf),
        in_specs=[SMEM] + [VMEM] * 4,
        out_specs=VMEM,
        compiler_params=PARAMS,
    )(place, arrived.reshape(slots, half), other.reshape(slots, half), w_gate, w_up)
    all_hidden = lax.all_gather(hidden, ("j", "k"), axis=0)
    piece = pl.pallas_call(
        down_kernel,
        out_shape=jax.ShapeDtypeStruct((slots, width), bf),
        in_specs=[SMEM] + [VMEM] * 5,
        out_specs=VMEM,
        compiler_params=PARAMS,
    )(place, all_hidden, w_down, moved[0], moved[1], swapped)
    back = lax.all_to_all(
        piece.reshape(dp_count, CAP, width), "dp", split_axis=0, concat_axis=0, tiled=True
    )
    spread = pl.pallas_call(
        spread_kernel,
        out_shape=jax.ShapeDtypeStruct((tok_rows, width), bf),
        in_specs=[SMEM, VMEM, VMEM],
        out_specs=VMEM,
        compiler_params=PARAMS,
    )(place, routes, back.reshape(slots, width))
    final = lax.all_to_all(
        spread.reshape(owners, tok_rows // owners, width),
        ("g", "j", "k"),
        split_axis=0,
        concat_axis=0,
        tiled=True,
    )
    return pl.pallas_call(
        finish_kernel,
        out_shape=jax.ShapeDtypeStruct((tok_rows // owners, model), bf),
        in_specs=[SMEM, VMEM, VMEM],
        out_specs=VMEM,
        compiler_params=PARAMS,
    )(place, scores, final.reshape(tok_rows, width))


def solution(mesh):
    dp_count, ctx_count = mesh.devices.shape
    split = Mesh(
        mesh.devices.reshape(dp_count, EXP_DP, ctx_count // EXP_DP // CORES, CORES),
        ("dp", "g", "j", "k"),
    )
    everywhere = ("dp", "g", "j", "k")
    in_specs = (
        P("dp", None),
        P("dp", None),
        P("dp", None),
        P(None, everywhere),
        P(None, everywhere),
        P(everywhere, None),
    )
    return jax.shard_map(
        per_device, mesh=split, in_specs=in_specs, out_specs=P(everywhere, None), check_vma=False
    )
```

time: 228 us -> 128 us (0.56)
  the two profiles are of different devices: /device:TPU:6 before, /device:TPU:8 now
where the time goes in v1:
time: 128 us
  starting transfers between devices  39.1 us (31%)
  waiting for transfers between devices  36.3 us (28%)
  blocking collectives  32.2 us (25%)
  local copies, waits for them, and re-layouts  10.7 us (8%)
  Pallas kernels  6.99 us (5%)
  other arithmetic  1.96 us (2%)
    all_to_all x1, blocking collectives, per_device(): lax.all_to_all(piece.reshape(dp_count, CAP, width), 'dp', split_axis=0, c...  21.7 us
    all_to_all x1, waiting for transfers between devices, per_device(): lax.all_to_all(spread.reshape(owners, tok_rows // owners, width), ('g', '...  19.1 us
    ppermute x2, waiting for transfers between devices, per_device(): lax.ppermute(columns(lax.rem(third + step, thirds)), 'j', [(i, (i + step)...  17.2 us
    all_to_all x1, starting transfers between devices, per_device(): lax.all_to_all(spread.reshape(owners, tok_rows // owners, width), ('g', '...  16 us
    all_to_all x1, starting transfers between devices, per_device(): lax.all_to_all(outgoing.reshape(dp_count, CAP, half), 'dp', split_axis=0,...  13 us
    all_gather x1, blocking collectives, per_device(): all_hidden = lax.all_gather(hidden, ('j', 'k'), axis=0)  10.5 us
    ppermute x2, starting transfers between devices, per_device(): lax.ppermute(columns(lax.rem(third + step, thirds)), 'j', [(i, (i + step)...  5.83 us
    unnamed x16, local copies, waits for them, and re-layouts  5.71 us
  transfers between devices with their start and end apart: 6, of which 3 were waited for; matrix products, arithmetic and copies ran while one was open for 5% of the time, Pallas kernels for 1%

profile of v1, /device:TPU:8, one launch (start us, length us, event | category | flops | bytes accessed | tf_op | source)
XLA Modules:
  0.0 127.6 jit_solution(15028380481100528348)
XLA Ops:
  0.0 0.8 copy.8.routes_ref
  0.8 0.1 pad_add_fusion.place_ref
  0.9 0.0 copy-start.1
  0.9 1.5 %copy-done.1 = bf16[192,5120]{1,0:T(8,128)(2,1)S(1)} copy-done((bf16[192,5120]{1,0:T(8,128)(2,1)S(1)}, bf16[192,5120]{1,0:T(8,128)(2,1)}, u32[]{:S(2)}) %copy-start.1) | copy-done | bytes 1966104
  2.4 1.0 shard_map.64
  3.4 0.0 copy-start.4
  3.4 0.6 copy-done.4
  4.0 0.0 copy-start
  4.0 1.0 reshape.21
  5.0 13.0 %all-to-all-start = ((bf16[32,4,2560]{2,1,0:T(4,128)(2,1)}), bf16[32,4,2560]{2,1,0:T(4,128)(2,1)S(1)}, u32[]{:S(2)}, u32[]{:S(2)}) async-start(bf16[32,4,2560]{2,1,0:T(4,128)(2,1)} %reshape.21), calls=%async_computation | async-start | bytes 1310720 | tf_op jit(solution)/shard_map/all_to_all | solution.py:163
  18.1 0.0 copy-done
  18.1 1.3 %constant_dynamic-slice_fusion = (bf16[128,1792]{1,0:T(8,128)(2,1)}, bf16[128,1792]{1,0:T(8,128)(2,1)}) fusion(bf16[128,5120]{1,0:T(8,128)(2,1)S(1)} %copy-done, s32[]{:T(128)S(6)} %select_n.19, s32[]{:T(128)S(6)} %select_n.18), kind=kLoop, calls=%fused_computation.4 | loop fusion | bytes 1835016 | tf_op jit(solution)/shard_map/dynamic_slice | solution.py:138
  19.4 3.2 %collective-permute-start.2 = (bf16[128,1792]{1,0:T(8,128)(2,1)}, bf16[128,1792]{1,0:T(8,128)(2,1)S(1)}, u32[]{:S(2)}, u32[]{:S(2)}) collective-permute-start(bf16[128,1792]{1,0:T(8,128)(2,1)} %get-tuple-element.5), channel_id=1, source_target_pairs={{0,4},{2,0},{4,2},{1,5},{3,1},{5,3},{6,10},{8,6},{10,8},{7,11},{9,... | collective-permute-start | bytes 1376264 | tf_op jit(solution)/shard_map/ppermute | solution.py:143
  22.7 2.6 %collective-permute-start.1 = (bf16[128,1792]{1,0:T(8,128)(2,1)}, bf16[128,1792]{1,0:T(8,128)(2,1)S(1)}, u32[]{:S(2)}, u32[]{:S(2)}) collective-permute-start(bf16[128,1792]{1,0:T(8,128)(2,1)} %get-tuple-element.6), channel_id=1, source_target_pairs={{0,2},{2,4},{4,0},{1,3},{3,5},{5,1},{6,8},{8,10},{10,6},{7,9},{9,1... | collective-permute-start | bytes 1376264 | tf_op jit(solution)/shard_map/ppermute | solution.py:143
  25.3 0.1 dynamic-slice_bitcast_fusion.2
  25.5 8.6 %collective-permute-done.2.last_ref = bf16[128,1792]{1,0:T(8,128)(2,1)S(1)} collective-permute-done((bf16[128,1792]{1,0:T(8,128)(2,1)}, bf16[128,1792]{1,0:T(8,128)(2,1)S(1)}, u32[]{:S(2)}, u32[]{:S(2)}) %collective-permute-start.2) | collective-permute-done | bytes 458784 | tf_op jit(solution)/shard_map/ppermute | solution.py:143
  34.0 8.6 %collective-permute-done.1.next_ref = bf16[128,1792]{1,0:T(8,128)(2,1)S(1)} collective-permute-done((bf16[128,1792]{1,0:T(8,128)(2,1)}, bf16[128,1792]{1,0:T(8,128)(2,1)S(1)}, u32[]{:S(2)}, u32[]{:S(2)}) %collective-permute-start.1) | collective-permute-done | bytes 458784 | tf_op jit(solution)/shard_map/ppermute | solution.py:143
  42.7 0.7 dynamic-slice_bitcast_fusion.1
  43.4 0.0 all-to-all-done
  43.4 1.9 %collective-permute-start = (bf16[32,4,2560]{2,1,0:T(4,128)(2,1)S(1)}, bf16[32,4,2560]{2,1,0:T(4,128)(2,1)}, u32[]{:S(2)}, u32[]{:S(2)}) collective-permute-start(bf16[32,4,2560]{2,1,0:T(4,128)(2,1)S(1)} %all-to-all-done), channel_id=1, source_target_pairs={{0,1},{1,0},{2,3},{3,2},{4,5},{5,4},{6,7},{7,6},{8,9},{9,8},{10,11... | collective-permute-start | bytes 1966088 | tf_op jit(solution)/shard_map/ppermute | solution.py:166
  45.3 1.9 %pad_maximum_fusion = bf16[3,128,896]{2,1,0:T(8,128)(2,1)} fusion(bf16[1,128,896]{2,1,0:T(8,128)(2,1)S(1)} %dynamic-slice_bitcast_fusion, bf16[1,128,896]{2,1,0:T(8,128)(2,1)} %dynamic-slice_bitcast_fusion.1, bf16[1,128,896]{2,1,0:T(8,128)(2,1)S(1)} %dynamic-slice_bitcast_fusion.2), kind=kLoop, calls=%fused_computation | loop fusion | flops 688128 | bytes 1376256 | tf_op jit(solution)/shard_map/stack | solution.py:151
  47.2 2.4 %collective-permute-start.3 = (bf16[3,128,896]{2,1,0:T(8,128)(2,1)}, bf16[3,128,896]{2,1,0:T(8,128)(2,1)}, u32[]{:S(2)}, u32[]{:S(2)}) collective-permute-start(bf16[3,128,896]{2,1,0:T(8,128)(2,1)} %pad_maximum_fusion), channel_id=1, source_target_pairs={{0,1},{1,0},{2,3},{3,2},{4,5},{5,4},{6,7},{7,6},{8,9},{9,8},{10,11... | collective-permute-start | bytes 2064392 | tf_op jit(solution)/shard_map/ppermute | solution.py:154
  49.6 0.1 reshape.22.own_ref
  49.7 0.0 collective-permute-done
  49.7 1.5 %reshape.23.other_ref = bf16[128,2560]{1,0:T(8,128)(2,1)S(1)} reshape(bf16[32,4,2560]{2,1,0:T(4,128)(2,1)} %collective-permute-done) | data formatting | bytes 1310720 | tf_op jit(solution)/shard_map/reshape | solution.py:173
  51.2 0.0 copy-start.2
  51.3 1.3 %copy-done.2 = bf16[5120,128]{1,0:T(8,128)(2,1)S(1)} copy-done((bf16[5120,128]{1,0:T(8,128)(2,1)S(1)}, bf16[5120,128]{1,0:T(8,128)(2,1)}, u32[]{:S(2)}) %copy-start.2) | copy-done | bytes 1310744
  52.6 0.0 copy-start.3
  52.6 1.3 %copy-done.3 = bf16[5120,128]{1,0:T(8,128)(2,1)S(1)} copy-done((bf16[5120,128]{1,0:T(8,128)(2,1)S(1)}, bf16[5120,128]{1,0:T(8,128)(2,1)}, u32[]{:S(2)}) %copy-start.3) | copy-done | bytes 1310744
  53.9 1.4 %shard_map.65 = bf16[128,128]{1,0:T(8,128)(2,1)S(1)} custom-call(s32[4]{0:T(128)S(1)} %pad_add_fusion.place_ref, bf16[128,2560]{1,0:T(8,128)(2,1)S(1)} %reshape.22.own_ref, bf16[128,2560]{1,0:T(8,128)(2,1)S(1)} %reshape.23.other_ref, bf16[5120,128]{1,0:T(8,128)(2,1)S(1)} %copy-done.2, bf16[5120,128]{1,0:T(8,128)(2,1)S(1)} %copy-done.3), custom_call_target="tpu_custom_call" | custom-call | tf_op jit(solution)/shard_map/pallas_call | solution.py:167
  55.3 10.5 %all-gather = bf16[768,128]{1,0:T(8,128)(2,1)S(1)} all-gather(bf16[128,128]{1,0:T(8,128)(2,1)S(1)} %shard_map.65), channel_id=2, replica_groups=mesh['dp'=32,'g'=4,'j'=3,'k'=2] {'j','k'}, dimensions={0}, use_global_device_ids=true | all-gather | bytes 229376 | tf_op jit(solution)/shard_map/all_gather | solution.py:174
  65.8 0.0 collective-permute-done.3.swap_ref
  65.8 1.6 %shard_map.66 = bf16[128,896]{1,0:T(8,128)(2,1)S(1)} custom-call(s32[4]{0:T(128)S(1)} %pad_add_fusion.place_ref, bf16[6,128,128]{2,1,0:T(8,128)(2,1)S(1)} %bitcast.14, bf16[128,5120]{1,0:T(8,128)(2,1)S(1)} %copy-done, bf16[128,1792]{1,0:T(8,128)(2,1)S(1)} %collective-permute-done.1.next_ref, bf16[128,1792]{1,0:T(8,128)(2,1)S(1)} %collective-permute-done.2.last_ref, ...), custom_call_target="tpu_custom_call" | custom-call | tf_op jit(solution)/shard_map/pallas_call | solution.py:175
  67.4 0.0 copy-start.5
  67.4 0.0 copy-start.6
  67.4 0.1 reshape.24
  67.5 21.7 %all_to_all.15 = bf16[32,4,896]{2,1,0:T(4,128)(2,1)S(1)} all-to-all(bf16[32,4,896]{2,1,0:T(4,128)(2,1)S(1)} %reshape.24), channel_id=1, replica_groups=mesh['dp'=32,'g'=4,'j'=3,'k'=2] {'dp'}, dimensions={0} | all-to-all | bytes 458752 | tf_op jit(solution)/shard_map/all_to_all | solution.py:182
  89.2 0.1 reshape.25.back_ref
  89.3 0.0 copy-done.5
  89.3 1.7 %shard_map.67 = bf16[192,896]{1,0:T(8,128)(2,1)} custom-call(s32[4]{0:T(128)S(1)} %pad_add_fusion.place_ref, s32[192,1]{1,0:T(8,128)S(1)} %copy-done.5, bf16[128,896]{1,0:T(8,128)(2,1)S(1)} %reshape.25.back_ref), custom_call_target="tpu_custom_call" | custom-call | tf_op jit(solution)/shard_map/pallas_call | solution.py:185
  91.0 16.0 %all-to-all-start.2 = ((bf16[24,8,896]{2,1,0:T(8,128)(2,1)}), bf16[24,8,896]{2,1,0:T(8,128)(2,1)S(1)}, u32[]{:S(2)}, u32[]{:S(2)}) async-start(bf16[24,8,896]{2,1,0:T(8,128)(2,1)} %bitcast.8), calls=%async_computation.2 | async-start | bytes 688128 | tf_op jit(solution)/shard_map/all_to_all | solution.py:192
  107.0 0.0 copy-done.6
  107.0 0.1 copy.9.scores_ref
  107.1 19.1 %all-to-all-done.2 = bf16[24,8,896]{2,1,0:T(8,128)(2,1)S(1)} async-done(((bf16[24,8,896]{2,1,0:T(8,128)(2,1)}), bf16[24,8,896]{2,1,0:T(8,128)(2,1)S(1)}, u32[]{:S(2)}, u32[]{:S(2)}) %all-to-all-start.2) | async-done | bytes 344096 | tf_op jit(solution)/shard_map/all_to_all | solution.py:192
  126.2 1.4 %shard_map.68 = bf16[8,5120]{1,0:T(8,128)(2,1)} custom-call(s32[4]{0:T(128)S(1)} %pad_add_fusion.place_ref, f32[192,8]{1,0:T(8,128)S(1)} %copy.9.scores_ref, bf16[192,896]{1,0:T(8,128)(2,1)S(1)} %bitcast.13), custom_call_target="tpu_custom_call" | custom-call | tf_op jit(solution)/shard_map/pallas_call | solution.py:199
  (1 shorter events, 0.0 us)
Async XLA Ops:
  0.9 1.5 %copy-start.1 = (bf16[192,5120]{1,0:T(8,128)(2,1)S(1)}, bf16[192,5120]{1,0:T(8,128)(2,1)}, u32[]{:S(2)}) copy-start(bf16[192,5120]{1,0:T(8,128)(2,1)} %tokens_ref.1) | copy-start | bytes 5898244
  3.4 0.6 copy-start.4
  4.0 14.0 %copy-start = (bf16[128,5120]{1,0:T(8,128)(2,1)S(1)}, bf16[128,5120]{1,0:T(8,128)(2,1)}, u32[]{:S(2)}) copy-start(bf16[128,5120]{1,0:T(8,128)(2,1)} %own_ref.1) | copy-start | bytes 3932164
  5.0 38.3 %all-to-all-start = ((bf16[32,4,2560]{2,1,0:T(4,128)(2,1)}), bf16[32,4,2560]{2,1,0:T(4,128)(2,1)S(1)}, u32[]{:S(2)}, u32[]{:S(2)}) async-start(bf16[32,4,2560]{2,1,0:T(4,128)(2,1)} %reshape.21), calls=%async_computation | async-start | bytes 1310720 | tf_op jit(solution)/shard_map/all_to_all | solution.py:163
  19.4 14.6 %collective-permute-start.2 = (bf16[128,1792]{1,0:T(8,128)(2,1)}, bf16[128,1792]{1,0:T(8,128)(2,1)S(1)}, u32[]{:S(2)}, u32[]{:S(2)}) collective-permute-start(bf16[128,1792]{1,0:T(8,128)(2,1)} %get-tuple-element.5), channel_id=1, source_target_pairs={{0,4},{2,0},{4,2},{1,5},{3,1},{5,3},{6,10},{8,6},{10,8},{7,11},{9,... | collective-permute-start | bytes 1376264 | tf_op jit(solution)/shard_map/ppermute | solution.py:143
  22.7 20.0 %collective-permute-start.1 = (bf16[128,1792]{1,0:T(8,128)(2,1)}, bf16[128,1792]{1,0:T(8,128)(2,1)S(1)}, u32[]{:S(2)}, u32[]{:S(2)}) collective-permute-start(bf16[128,1792]{1,0:T(8,128)(2,1)} %get-tuple-element.6), channel_id=1, source_target_pairs={{0,2},{2,4},{4,0},{1,3},{3,5},{5,1},{6,8},{8,10},{10,6},{7,9},{9,1... | collective-permute-start | bytes 1376264 | tf_op jit(solution)/shard_map/ppermute | solution.py:143
  43.4 6.4 %collective-permute-start = (bf16[32,4,2560]{2,1,0:T(4,128)(2,1)S(1)}, bf16[32,4,2560]{2,1,0:T(4,128)(2,1)}, u32[]{:S(2)}, u32[]{:S(2)}) collective-permute-start(bf16[32,4,2560]{2,1,0:T(4,128)(2,1)S(1)} %all-to-all-done), channel_id=1, source_target_pairs={{0,1},{1,0},{2,3},{3,2},{4,5},{5,4},{6,7},{7,6},{8,9},{9,8},{10,11... | collective-permute-start | bytes 1966088 | tf_op jit(solution)/shard_map/ppermute | solution.py:166
  47.2 18.6 %collective-permute-start.3 = (bf16[3,128,896]{2,1,0:T(8,128)(2,1)}, bf16[3,128,896]{2,1,0:T(8,128)(2,1)}, u32[]{:S(2)}, u32[]{:S(2)}) collective-permute-start(bf16[3,128,896]{2,1,0:T(8,128)(2,1)} %pad_maximum_fusion), channel_id=1, source_target_pairs={{0,1},{1,0},{2,3},{3,2},{4,5},{5,4},{6,7},{7,6},{8,9},{9,8},{10,11... | collective-permute-start | bytes 2064392 | tf_op jit(solution)/shard_map/ppermute | solution.py:154
  51.2 1.3 %copy-start.2 = (bf16[5120,128]{1,0:T(8,128)(2,1)S(1)}, bf16[5120,128]{1,0:T(8,128)(2,1)}, u32[]{:S(2)}) copy-start(bf16[5120,128]{1,0:T(8,128)(2,1)} %gate_ref.1) | copy-start | bytes 3932164
  52.6 1.3 %copy-start.3 = (bf16[5120,128]{1,0:T(8,128)(2,1)S(1)}, bf16[5120,128]{1,0:T(8,128)(2,1)}, u32[]{:S(2)}) copy-start(bf16[5120,128]{1,0:T(8,128)(2,1)} %up_ref.1) | copy-start | bytes 3932164
  67.4 21.9 %copy-start.5 = (s32[192,1]{1,0:T(8,128)S(1)}, s32[192,1]{1,0:T(8,128)}, u32[]{:S(2)}) copy-start(s32[192,1]{1,0:T(8,128)} %copy-done.4) | copy-start | bytes 2308
  67.4 39.5 %copy-start.6 = (f32[192,8]{0,1:T(8,128)S(1)}, f32[192,8]{0,1:T(8,128)}, u32[]{:S(2)}) copy-start(f32[192,8]{0,1:T(8,128)} %param.7) | copy-start | bytes 18436
  91.0 35.2 %all-to-all-start.2 = ((bf16[24,8,896]{2,1,0:T(8,128)(2,1)}), bf16[24,8,896]{2,1,0:T(8,128)(2,1)S(1)}, u32[]{:S(2)}, u32[]{:S(2)}) async-start(bf16[24,8,896]{2,1,0:T(8,128)(2,1)} %bitcast.8), calls=%async_computation.2 | async-start | bytes 688128 | tf_op jit(solution)/shard_map/all_to_all | solution.py:192

commit v2 on v0

v2 whole, which is shorter than its diff:
```python
import functools

import jax
import jax.numpy as jnp
from jax import lax
from jax.experimental import pallas as pl
from jax.experimental.pallas import tpu as pltpu
from jax.sharding import Mesh
from jax.sharding import PartitionSpec as P

EXP_DP = 4
CAP = 4
CORES = 2
LANES = 128
QUARTERS = 4
CHUNK = CAP * QUARTERS
ROUTE_SCALE = 2.5
VMEM_LIMIT = 20 * 1024 * 1024
FAR = 1 << 20
BESIDE = pl.CostEstimate(flops=8 * 10**9, bytes_accessed=16 * 1024 * 1024, transcendentals=0)

VMEM = pl.BlockSpec(memory_space=pltpu.VMEM)
HBM = pl.BlockSpec(memory_space=pltpu.HBM)


def iota(shape, axis):
    return lax.broadcasted_iota(jnp.int32, shape, axis)


def one_hot(mask):
    return jnp.where(mask, 1.0, 0.0).astype(jnp.bfloat16)


def dot(a, b):
    return jnp.dot(a, b, preferred_element_type=jnp.float32)


def slots_of_tokens(routes, group, down):
    tokens = routes.shape[1]
    row, col = iota((tokens, tokens), 0), iota((tokens, tokens), 1)
    across = jnp.broadcast_to(routes, (tokens, tokens))
    column = jnp.sum(jnp.where(row == col, across, 0), axis=1, keepdims=True)
    same = across == column
    if down:
        rank = jnp.sum((same & (col < row)).astype(jnp.int32), axis=1, keepdims=True)
        own = column
    else:
        rank = jnp.sum((same & (row < col)).astype(jnp.int32), axis=0, keepdims=True)
        own = routes
    slot = (own >> 2) * CAP + rank
    return jnp.where((own & 3) == group, slot, jnp.int32(FAR))


def pick_kernel(routes_ref, tokens_ref, out_ref, row_ref, half_ref, sems):
    rows, width = out_ref.shape
    base = lax.axis_index("k") * (QUARTERS * width)
    copies = [pltpu.make_async_copy(routes_ref, row_ref, sems.at[QUARTERS])]
    for q in range(QUARTERS):
        start = pl.multiple_of(base + q * width, LANES)
        copies.append(
            pltpu.make_async_copy(
                tokens_ref.at[:, pl.ds(start, width)], half_ref.at[q], sems.at[q]
            )
        )
    for copy in copies:
        copy.start()
    copies[0].wait()
    slot = slots_of_tokens(row_ref[...], lax.axis_index("g"), False)
    row = iota((rows, 1), 0)
    wanted = (row >> 4) * CAP + (row & 3)
    total = None
    for q in range(QUARTERS):
        pick = one_hot(jnp.where(((row >> 2) & 3) == q, wanted, -1) == slot)
        copies[1 + q].wait()
        term = dot(pick, half_ref[q])
        total = term if total is None else total + term
    out_ref[...] = total.astype(jnp.bfloat16)


def run(copies):
    for copy in copies:
        copy.start()
    for copy in copies:
        copy.wait()


def away_kernel(down_ref, out_ref, sem):
    half = out_ref.shape[1]
    start = pl.multiple_of((1 - lax.axis_index("k")) * half, LANES)
    run([pltpu.make_async_copy(down_ref.at[:, pl.ds(start, half)], out_ref, sem)])


def blocks_kernel(down_ref, given_ref, *rest):
    blocks, sems = rest[:-1], rest[-1]
    half = given_ref.shape[1]
    copies = []
    for step, block_ref in enumerate(blocks):
        width = block_ref.shape[2]
        start = jnp.minimum(lax.rem(lax.axis_index("j") + step, 3) * width, half - width)
        starts = (lax.axis_index("k") * half + start, start)
        for which, (ref, at) in enumerate(zip((down_ref, given_ref), starts)):
            copies.append(
                pltpu.make_async_copy(
                    ref.at[:, pl.ds(pl.multiple_of(at, LANES), width)],
                    block_ref.at[which],
                    sems.at[CORES * step + which],
                )
            )
    run(copies)


def join_kernel(own, gate_ref, up_ref, out_ref, sems):
    half, units = out_ref.shape[0], gate_ref.shape[1]
    me = lax.axis_index("k")
    start = pl.multiple_of((me if own else 1 - me) * half, LANES)
    run(
        [
            pltpu.make_async_copy(
                w_ref.at[pl.ds(start, half)], out_ref.at[:, pl.ds(at * units, units)], sems.at[at]
            )
            for at, w_ref in enumerate((gate_ref, up_ref))
        ]
    )


def unpack(slots, rows, q):
    slot, row = iota((slots, rows), 0), iota((slots, rows), 1)
    return one_hot(row == (slot >> 2) * CHUNK + q * CAP + (slot & 3))


def project(chunks_ref, weights_ref, slots):
    rows, width = chunks_ref.shape
    chunks = chunks_ref[...]
    total = None
    for q in range(QUARTERS):
        part = dot(unpack(slots, rows, q), chunks).astype(jnp.bfloat16)
        term = dot(part, weights_ref[q * width : (q + 1) * width, :])
        total = term if total is None else total + term
    return total


def own_kernel(chunks_ref, weights_ref, out_ref):
    out_ref[...] = project(chunks_ref, weights_ref, out_ref.shape[0])


def hidden_kernel(partial_ref, chunks_ref, weights_ref, out_ref):
    slots, units = out_ref.shape
    pre = partial_ref[...] + project(chunks_ref, weights_ref, slots)
    gate, up = pre[:, :units], pre[:, units:]
    out_ref[...] = (gate * jax.nn.sigmoid(gate) * up).astype(jnp.bfloat16)


def down_kernel(hidden_ref, kept_ref, next_ref, last_ref, out_ref):
    slots = hidden_ref.shape[1]
    rows, width = out_ref.shape
    columns = next_ref.shape[2]
    third, core = lax.axis_index("j"), lax.axis_index("k")
    total = None
    for step, weights in enumerate((kept_ref, next_ref, last_ref)):
        source = lax.rem(third + 3 - step, 3)
        for which in range(CORES):
            who = core if which == 0 else 1 - core
            term = dot(hidden_ref[CORES * source + who], weights[which])
            total = term if total is None else total + term
    piece = total.astype(jnp.bfloat16)
    out = None
    row, slot = iota((rows, slots), 0), iota((rows, slots), 1)
    hit = slot == (row >> 4) * CAP + (row & 3)
    for q in range(QUARTERS):
        block = piece[:, q * width : min(columns, (q + 1) * width)]
        if block.shape[1] < width:
            block = jnp.concatenate(
                [block, jnp.zeros((slots, width - block.shape[1]), block.dtype)], axis=1
            )
        term = dot(one_hot(hit & (((row >> 2) & 3) == q)), block)
        out = term if out is None else out + term
    out_ref[...] = out.astype(jnp.bfloat16)


def spread_kernel(routes_ref, back_ref, out_ref):
    rows, width = back_ref.shape
    tokens, columns = out_ref.shape
    slot = slots_of_tokens(routes_ref[...], lax.axis_index("g"), True)
    first = (slot >> 2) * CHUNK + (slot & 3)
    row = iota((tokens, rows), 1)
    back = back_ref[...]
    for q in range(QUARTERS):
        stop = min(columns, (q + 1) * width)
        block = dot(one_hot(row == first + q * CAP), back[:, : stop - q * width])
        out_ref[:, q * width : stop] = block.astype(jnp.bfloat16)


def finish_kernel(scores_ref, parts_ref, out_ref):
    rows, model = out_ref.shape
    width = parts_ref.shape[1]
    tokens = scores_ref.shape[1]
    sig = jax.nn.sigmoid(scores_ref[...])
    gates = ROUTE_SCALE * sig[:1] / jnp.sum(sig, axis=0, keepdims=True)
    owner = (lax.axis_index("g") * lax.axis_size("j") + lax.axis_index("j")) * CORES
    owner += lax.axis_index("k")
    mine = iota((rows, tokens), 1) == owner * rows + iota((rows, tokens), 0)
    gates = jnp.sum(jnp.where(mine, gates, 0.0), axis=1, keepdims=True)
    parts = parts_ref[...].astype(jnp.float32)
    per_group = parts.shape[0] // EXP_DP
    total = parts[:per_group]
    for group in range(1, EXP_DP):
        total = total + parts[group * per_group : (group + 1) * per_group]
    half = model // CORES
    for part in range(per_group // rows):
        third, core = part // CORES, part % CORES
        base = min(third * width, half - width)
        skip = third * width - base
        block = total[part * rows : (part + 1) * rows, skip:] * gates
        base += core * half
        out_ref[:, base + skip : base + width] = block.astype(jnp.bfloat16)


def call(kernel, shapes, in_specs, args, limit=VMEM_LIMIT, **more):
    single = not isinstance(shapes, list)
    return pl.pallas_call(
        kernel,
        out_shape=shapes,
        in_specs=in_specs,
        out_specs=VMEM if single else [VMEM] * len(shapes),
        compiler_params=pltpu.CompilerParams(vmem_limit_bytes=limit),
        **more,
    )(*args)


def in_hbm(x):
    return pltpu.with_memory_space_constraint(x, pltpu.HBM)


def exchange(x):
    return lax.ppermute(x, "k", [(0, 1), (1, 0)])


def over_dp(x):
    return lax.all_to_all(x, "dp", split_axis=0, concat_axis=0, tiled=True)


def per_device(tokens, scores, routes, w_gate, w_up, w_down):
    dp_count = lax.axis_size("dp")
    tok_rows, model = tokens.shape
    units = w_down.shape[0]
    thirds = lax.axis_size("j")
    owners = EXP_DP * thirds * CORES
    slots = dp_count * CAP
    half = model // CORES
    width = -(-model // (thirds * CORES * LANES)) * LANES
    quarter = -(-width // (QUARTERS * LANES)) * LANES
    bf, f32 = jnp.bfloat16, jnp.float32
    routes_row, scores_row = routes.reshape(1, tok_rows), scores.T

    def array(shape, dtype=bf):
        return jax.ShapeDtypeStruct(shape, dtype)

    flat = (dp_count * CHUNK, half // QUARTERS)
    outgoing = call(
        pick_kernel,
        array(flat),
        [HBM, HBM],
        (in_hbm(routes_row), in_hbm(tokens)),
        scratch_shapes=[
            pltpu.VMEM((1, tok_rows), jnp.int32),
            pltpu.VMEM((QUARTERS, tok_rows, half // QUARTERS), bf),
            pltpu.SemaphoreType.DMA((QUARTERS + 1,)),
        ],
    )
    arrived = over_dp(outgoing.reshape(dp_count, CHUNK, half // QUARTERS))
    away = call(
        away_kernel,
        array((units, half)),
        [HBM],
        (w_down,),
        scratch_shapes=[pltpu.SemaphoreType.DMA],
    )
    given = exchange(away)
    kept, *sent = call(
        blocks_kernel,
        [pltpu.HBM((CORES, units, width), bf)] + [array((CORES, units, width))] * (thirds - 1),
        [HBM, HBM],
        (w_down, given),
        scratch_shapes=[pltpu.SemaphoreType.DMA((CORES * thirds,))],
    )
    arrived = lax.optimization_barrier((arrived, sent))[0]
    moved = [
        lax.ppermute(block, "j", [(i, (i + step) % thirds) for i in range(thirds)])
        for step, block in enumerate(sent, 1)
    ]
    other = exchange(arrived)

    def joined(own, after):
        gate, up, _ = lax.optimization_barrier((w_gate, w_up, after))
        return call(
            functools.partial(join_kernel, own),
            pltpu.VMEM((half, 2 * units), bf),
            [HBM, HBM],
            (in_hbm(gate), in_hbm(up)),
            scratch_shapes=[pltpu.SemaphoreType.DMA((2,))],
            cost_estimate=None if own else BESIDE,
        )

    other = exchange(arrived)
    partial = call(
        own_kernel,
        array((slots, 2 * units), f32),
        [VMEM] * 2,
        (arrived.reshape(flat), joined(True, sent)),
        cost_estimate=BESIDE,
    )
    hidden = call(
        hidden_kernel,
        array((slots, units)),
        [VMEM] * 3,
        (partial, other.reshape(flat), joined(False, partial)),
    )
    all_hidden = lax.all_gather(hidden, ("j", "k"), axis=0)
    piece = call(
        down_kernel,
        array((dp_count * CHUNK, quarter)),
        [VMEM] * (1 + thirds),
        (all_hidden, kept, *moved),
    )
    back = over_dp(piece.reshape(dp_count, CHUNK, quarter))
    spread = call(
        spread_kernel,
        array((tok_rows, width)),
        [VMEM, VMEM],
        (routes_row, back.reshape(dp_count * CHUNK, quarter)),
    )
    final = lax.all_to_all(
        spread.reshape(owners, tok_rows // owners, width),
        ("g", "j", "k"),
        split_axis=0,
        concat_axis=0,
        tiled=True,
    )
    return call(
        finish_kernel,
        array((tok_rows // owners, model)),
        [VMEM, VMEM],
        (scores_row, final.reshape(tok_rows, width)),
    )


def solution(mesh):
    dp_count, ctx_count = mesh.devices.shape
    split = Mesh(
        mesh.devices.reshape(dp_count, EXP_DP, ctx_count // EXP_DP // CORES, CORES),
        ("dp", "g", "j", "k"),
    )
    everywhere = ("dp", "g", "j", "k")
    in_specs = (
        P("dp", None),
        P("dp", None),
        P("dp", None),
        P(None, everywhere),
        P(None, everywhere),
        P(everywhere, None),
    )
    return jax.shard_map(
        per_device, mesh=split, in_specs=in_specs, out_specs=P(everywhere, None), check_vma=False
    )
```

time: 228 us -> 110 us (0.48)
  the two profiles are of different devices: /device:TPU:6 before, /device:TPU:8 now
where the time goes in v2:
time: 110 us; the launch traced here: 109 us
  blocking collectives  67.7 us (62%)
  starting transfers between devices  23.7 us (22%)
  Pallas kernels  11.4 us (10%)
  waiting for transfers between devices  6.37 us (6%)
    all_to_all x1, blocking collectives, per_device(): lax.all_to_all(spread.reshape(owners, tok_rows // owners, width), ('g', '...  33.6 us
    all_to_all x1, blocking collectives, over_dp(): return lax.all_to_all(x, 'dp', split_axis=0, concat_axis=0, tiled=True)  22.2 us
    all_to_all x1, starting transfers between devices, over_dp(): return lax.all_to_all(x, 'dp', split_axis=0, concat_axis=0, tiled=True)  13.2 us
    all_gather x1, blocking collectives, per_device(): all_hidden = lax.all_gather(hidden, ('j', 'k'), axis=0)  11.8 us
    pallas_call x10, Pallas kernels, call(): pl.pallas_call(kernel, out_shape=shapes, in_specs=in_specs, out_specs=VME...  11.4 us
    ppermute x2, starting transfers between devices, per_device(): lax.ppermute(block, 'j', [(i, (i + step) % thirds) for i in range(thirds)])  6.74 us
    all_to_all x1, waiting for transfers between devices, over_dp(): return lax.all_to_all(x, 'dp', split_axis=0, concat_axis=0, tiled=True)  4.29 us
    ppermute x2, starting transfers between devices, exchange(): return lax.ppermute(x, 'k', [(0, 1), (1, 0)])  3.83 us
  transfers between devices with their start and end apart: 5, of which 2 were waited for; matrix products, arithmetic and copies ran while one was open for 0% of the time, Pallas kernels for 5%

profile of v2, /device:TPU:8, one launch (start us, length us, event | category | flops | bytes accessed | tf_op | source)
XLA Modules:
  0.0 109.3 jit_solution(15462938786784468645)
XLA Ops:
  0.0 3.3 %shard_map.64 = bf16[512,640]{1,0:T(8,128)(2,1)} custom-call(s32[1,192]{1,0:T(1,128)} %bitcast.18, bf16[192,5120]{1,0:T(8,128)(2,1)} %tokens_ref.1), custom_call_target="tpu_custom_call" | custom-call | tf_op jit(solution)/shard_map/pallas_call | solution.py:220
  3.3 0.0 copy-start
  3.3 13.2 %all-to-all-start = ((bf16[32,16,640]{2,1,0:T(8,128)(2,1)}), bf16[32,16,640]{2,1,0:T(8,128)(2,1)S(1)}, u32[]{:S(2)}, u32[]{:S(2)}) async-start(bf16[32,16,640]{2,1,0:T(8,128)(2,1)} %bitcast.2), calls=%async_computation | async-start | bytes 1310720 | tf_op jit(solution)/shard_map/all_to_all | solution.py:239
  16.5 0.0 copy-done
  16.5 0.1 shard_map.65
  16.6 1.9 %collective-permute-start = (bf16[128,2560]{1,0:T(8,128)(2,1)S(1)}, bf16[128,2560]{1,0:T(8,128)(2,1)S(1)}, u32[]{:S(2)}, u32[]{:S(2)}) collective-permute-start(bf16[128,2560]{1,0:T(8,128)(2,1)S(1)} %shard_map.65), channel_id=1, source_target_pairs={{0,1},{1,0},{2,3},{3,2},{4,5},{5,4},{6,7},{7,6},{8,9},{9,8},{10,11... | collective-permute-start | bytes 1966088 | tf_op jit(solution)/shard_map/ppermute | solution.py:235
  18.5 2.1 %collective-permute-done.given_ref = bf16[128,2560]{1,0:T(8,128)(2,1)S(1)} collective-permute-done((bf16[128,2560]{1,0:T(8,128)(2,1)S(1)}, bf16[128,2560]{1,0:T(8,128)(2,1)S(1)}, u32[]{:S(2)}, u32[]{:S(2)}) %collective-permute-start) | collective-permute-done | bytes 655392 | tf_op jit(solution)/shard_map/ppermute | solution.py:235
  20.5 1.2 %shard_map.66 = (bf16[2,128,896]{2,1,0:T(8,128)(2,1)}, bf16[2,128,896]{2,1,0:T(8,128)(2,1)}, bf16[2,128,896]{2,1,0:T(8,128)(2,1)S(1)}) custom-call(bf16[128,5120]{1,0:T(8,128)(2,1)S(1)} %copy-done, bf16[128,2560]{1,0:T(8,128)(2,1)S(1)} %collective-permute-done.given_ref), custom_call_target="tpu_custom_call" | custom-call | tf_op jit(solution)/shard_map/pallas_call | solution.py:220
  21.7 1.9 %collective-permute-start.2 = (bf16[2,128,896]{2,1,0:T(8,128)(2,1)}, bf16[2,128,896]{2,1,0:T(8,128)(2,1)S(1)}, u32[]{:S(2)}, u32[]{:S(2)}) collective-permute-start(bf16[2,128,896]{2,1,0:T(8,128)(2,1)} %get-tuple-element.13), channel_id=1, source_target_pairs={{0,2},{2,4},{4,0},{1,3},{3,5},{5,1},{6,8},{8,10},{10,6},{7,9},{9,1... | collective-permute-start | bytes 1376264 | tf_op jit(solution)/shard_map/ppermute | solution.py:288
  23.7 4.8 %collective-permute-start.3 = (bf16[2,128,896]{2,1,0:T(8,128)(2,1)S(1)}, bf16[2,128,896]{2,1,0:T(8,128)(2,1)S(1)}, u32[]{:S(2)}, u32[]{:S(2)}) collective-permute-start(bf16[2,128,896]{2,1,0:T(8,128)(2,1)S(1)} %get-tuple-element.14), channel_id=1, source_target_pairs={{0,4},{2,0},{4,2},{1,5},{3,1},{5,3},{6,10},{8,6},{10,8},{7,11},{9,... | collective-permute-start | bytes 1376264 | tf_op jit(solution)/shard_map/ppermute | solution.py:288
  28.5 1.3 %shard_map.67.weights_ref = bf16[2560,256]{1,0:T(8,128)(2,1)S(1)} custom-call(bf16[5120,128]{1,0:T(8,128)(2,1)} %gate_ref.1, bf16[5120,128]{1,0:T(8,128)(2,1)} %up_ref.1), custom_call_target="tpu_custom_call" | custom-call | tf_op jit(solution)/shard_map/pallas_call | solution.py:220
  29.8 4.3 %all-to-all-done = bf16[32,16,640]{2,1,0:T(8,128)(2,1)S(1)} async-done(((bf16[32,16,640]{2,1,0:T(8,128)(2,1)}), bf16[32,16,640]{2,1,0:T(8,128)(2,1)S(1)}, u32[]{:S(2)}, u32[]{:S(2)}) %all-to-all-start) | async-done | bytes 655392 | tf_op jit(solution)/shard_map/all_to_all | solution.py:239
  34.1 1.9 %collective-permute-start.1 = (bf16[32,16,640]{2,1,0:T(8,128)(2,1)S(1)}, bf16[32,16,640]{2,1,0:T(8,128)(2,1)S(1)}, u32[]{:S(2)}, u32[]{:S(2)}) collective-permute-start(bf16[32,16,640]{2,1,0:T(8,128)(2,1)S(1)} %all-to-all-done), channel_id=1, source_target_pairs={{0,1},{1,0},{2,3},{3,2},{4,5},{5,4},{6,7},{7,6},{8,9},{9,8},{10,11... | collective-permute-start | bytes 1966088 | tf_op jit(solution)/shard_map/ppermute | solution.py:235
  36.0 0.9 shard_map.68.partial_ref
  37.0 1.3 %shard_map.69.weights_ref = bf16[2560,256]{1,0:T(8,128)(2,1)S(1)} custom-call(bf16[5120,128]{1,0:T(8,128)(2,1)} %gate_ref.1, bf16[5120,128]{1,0:T(8,128)(2,1)} %up_ref.1), custom_call_target="tpu_custom_call" | custom-call | flops 8000000000 | bytes 16777216 | tf_op jit(solution)/shard_map/pallas_call | solution.py:220
  38.3 0.0 copy-start.1
  38.3 0.0 collective-permute-done.1
  38.3 1.0 shard_map.70
  39.3 0.0 copy-start.3
  39.3 11.8 %all-gather = bf16[768,128]{1,0:T(8,128)(2,1)S(1)} all-gather(bf16[128,128]{1,0:T(8,128)(2,1)S(1)} %shard_map.70), channel_id=2, replica_groups=mesh['dp'=32,'g'=4,'j'=3,'k'=2] {'j','k'}, dimensions={0}, use_global_device_ids=true | all-gather | bytes 229376 | tf_op jit(solution)/shard_map/all_gather | solution.py:318
  51.1 0.0 collective-permute-done.2.next_ref
  51.1 0.0 collective-permute-done.3.last_ref
  51.1 0.0 copy-done.1
  51.1 0.9 shard_map.71
  52.1 0.0 copy-start.2
  52.1 22.2 %all_to_all.15 = bf16[32,16,256]{2,1,0:T(8,128)(2,1)S(1)} all-to-all(bf16[32,16,256]{2,1,0:T(8,128)(2,1)S(1)} %bitcast.12), channel_id=1, replica_groups=mesh['dp'=32,'g'=4,'j'=3,'k'=2] {'dp'}, dimensions={0} | all-to-all | bytes 524288 | tf_op jit(solution)/shard_map/all_to_all | solution.py:239
  74.3 0.0 copy-done.3
  74.3 0.6 shard_map.72
  74.9 33.6 %all_to_all.16 = bf16[24,8,896]{2,1,0:T(8,128)(2,1)S(1)} all-to-all(bf16[24,8,896]{2,1,0:T(8,128)(2,1)S(1)} %bitcast.10), channel_id=1, replica_groups=mesh['dp'=32,'g'=4,'j'=3,'k'=2] {'g','j','k'}, dimensions={0} | all-to-all | bytes 688128 | tf_op jit(solution)/shard_map/all_to_all | solution.py:332
  108.5 0.0 copy-done.2
  108.5 0.7 shard_map.73
Async XLA Ops:
  3.3 13.2 %copy-start = (bf16[128,5120]{1,0:T(8,128)(2,1)S(1)}, bf16[128,5120]{1,0:T(8,128)(2,1)}, u32[]{:S(2)}) copy-start(bf16[128,5120]{1,0:T(8,128)(2,1)} %down_ref.3) | copy-start | bytes 3932164
  3.3 30.8 %all-to-all-start = ((bf16[32,16,640]{2,1,0:T(8,128)(2,1)}), bf16[32,16,640]{2,1,0:T(8,128)(2,1)S(1)}, u32[]{:S(2)}, u32[]{:S(2)}) async-start(bf16[32,16,640]{2,1,0:T(8,128)(2,1)} %bitcast.2), calls=%async_computation | async-start | bytes 1310720 | tf_op jit(solution)/shard_map/all_to_all | solution.py:239
  16.6 4.0 %collective-permute-start = (bf16[128,2560]{1,0:T(8,128)(2,1)S(1)}, bf16[128,2560]{1,0:T(8,128)(2,1)S(1)}, u32[]{:S(2)}, u32[]{:S(2)}) collective-permute-start(bf16[128,2560]{1,0:T(8,128)(2,1)S(1)} %shard_map.65), channel_id=1, source_target_pairs={{0,1},{1,0},{2,3},{3,2},{4,5},{5,4},{6,7},{7,6},{8,9},{9,8},{10,11... | collective-permute-start | bytes 1966088 | tf_op jit(solution)/shard_map/ppermute | solution.py:235
  21.7 29.4 %collective-permute-start.2 = (bf16[2,128,896]{2,1,0:T(8,128)(2,1)}, bf16[2,128,896]{2,1,0:T(8,128)(2,1)S(1)}, u32[]{:S(2)}, u32[]{:S(2)}) collective-permute-start(bf16[2,128,896]{2,1,0:T(8,128)(2,1)} %get-tuple-element.13), channel_id=1, source_target_pairs={{0,2},{2,4},{4,0},{1,3},{3,5},{5,1},{6,8},{8,10},{10,6},{7,9},{9,1... | collective-permute-start | bytes 1376264 | tf_op jit(solution)/shard_map/ppermute | solution.py:288
  23.7 27.5 %collective-permute-start.3 = (bf16[2,128,896]{2,1,0:T(8,128)(2,1)S(1)}, bf16[2,128,896]{2,1,0:T(8,128)(2,1)S(1)}, u32[]{:S(2)}, u32[]{:S(2)}) collective-permute-start(bf16[2,128,896]{2,1,0:T(8,128)(2,1)S(1)} %get-tuple-element.14), channel_id=1, source_target_pairs={{0,4},{2,0},{4,2},{1,5},{3,1},{5,3},{6,10},{8,6},{10,8},{7,11},{9,... | collective-permute-start | bytes 1376264 | tf_op jit(solution)/shard_map/ppermute | solution.py:288
  34.1 4.2 %collective-permute-start.1 = (bf16[32,16,640]{2,1,0:T(8,128)(2,1)S(1)}, bf16[32,16,640]{2,1,0:T(8,128)(2,1)S(1)}, u32[]{:S(2)}, u32[]{:S(2)}) collective-permute-start(bf16[32,16,640]{2,1,0:T(8,128)(2,1)S(1)} %all-to-all-done), channel_id=1, source_target_pairs={{0,1},{1,0},{2,3},{3,2},{4,5},{5,4},{6,7},{7,6},{8,9},{9,8},{10,11... | collective-permute-start | bytes 1966088 | tf_op jit(solution)/shard_map/ppermute | solution.py:235
  38.3 12.8 %copy-start.1 = (bf16[2,128,896]{2,1,0:T(8,128)(2,1)S(1)}, bf16[2,128,896]{2,1,0:T(8,128)(2,1)}, u32[]{:S(2)}) copy-start(bf16[2,128,896]{2,1,0:T(8,128)(2,1)} %get-tuple-element.20.kept_ref) | copy-start | bytes 1376260
  39.3 35.0 %copy-start.3 = (s32[192,1]{0,1:T(1,128)S(1)}, s32[192,1]{0,1:T(1,128)}, u32[]{:S(2)}) copy-start(s32[192,1]{0,1:T(1,128)} %param.8) | copy-start | bytes 2308
  52.1 56.5 %copy-start.2 = (f32[192,8]{0,1:T(8,128)S(1)}, f32[192,8]{0,1:T(8,128)}, u32[]{:S(2)}) copy-start(f32[192,8]{0,1:T(8,128)} %param.7) | copy-start | bytes 18436

commit v3 on v2

--- a/solution.py
+++ b/solution.py
@@ -53,13 +53,15 @@
 
 def pick_kernel(routes_ref, tokens_ref, out_ref, row_ref, half_ref, sems):
     rows, width = out_ref.shape
-    base = lax.axis_index("k") * (QUARTERS * width)
-    copies = [pltpu.make_async_copy(routes_ref, row_ref, sems.at[QUARTERS])]
-    for q in range(QUARTERS):
-        start = pl.multiple_of(base + q * width, LANES)
+    tokens, half = half_ref.shape
+    start = pl.multiple_of(lax.axis_index("k") * half, LANES)
+    part = tokens // 2
+    copies = [pltpu.make_async_copy(routes_ref, row_ref, sems.at[2])]
+    for at in range(2):
+        span = pl.ds(at * part, part)
         copies.append(
             pltpu.make_async_copy(
-                tokens_ref.at[:, pl.ds(start, width)], half_ref.at[q], sems.at[q]
+                tokens_ref.at[span, pl.ds(start, half)], half_ref.at[span], sems.at[at]
             )
         )
     for copy in copies:
@@ -68,11 +70,14 @@
     slot = slots_of_tokens(row_ref[...], lax.axis_index("g"), False)
     row = iota((rows, 1), 0)
     wanted = (row >> 4) * CAP + (row & 3)
+    picks = [
+        one_hot(jnp.where(((row >> 2) & 3) == q, wanted, -1) == slot) for q in range(QUARTERS)
+    ]
+    for copy in copies[1:]:
+        copy.wait()
     total = None
     for q in range(QUARTERS):
-        pick = one_hot(jnp.where(((row >> 2) & 3) == q, wanted, -1) == slot)
-        copies[1 + q].wait()
-        term = dot(pick, half_ref[q])
+        term = dot(picks[q], half_ref[:, q * width : (q + 1) * width])
         total = term if total is None else total + term
     out_ref[...] = total.astype(jnp.bfloat16)
 
@@ -84,28 +89,17 @@
         copy.wait()
 
 
-def away_kernel(down_ref, out_ref, sem):
-    half = out_ref.shape[1]
-    start = pl.multiple_of((1 - lax.axis_index("k")) * half, LANES)
-    run([pltpu.make_async_copy(down_ref.at[:, pl.ds(start, half)], out_ref, sem)])
-
-
-def blocks_kernel(down_ref, given_ref, *rest):
+def blocks_kernel(down_ref, *rest):
     blocks, sems = rest[:-1], rest[-1]
-    half = given_ref.shape[1]
+    model = down_ref.shape[1]
     copies = []
-    for step, block_ref in enumerate(blocks):
-        width = block_ref.shape[2]
-        start = jnp.minimum(lax.rem(lax.axis_index("j") + step, 3) * width, half - width)
-        starts = (lax.axis_index("k") * half + start, start)
-        for which, (ref, at) in enumerate(zip((down_ref, given_ref), starts)):
-            copies.append(
-                pltpu.make_async_copy(
-                    ref.at[:, pl.ds(pl.multiple_of(at, LANES), width)],
-                    block_ref.at[which],
-                    sems.at[CORES * step + which],
-                )
-            )
+    for at, block_ref in enumerate(blocks):
+        width = block_ref.shape[1]
+        to = lax.rem(lax.axis_index("j") + at + 1, 3)
+        start = pl.multiple_of(jnp.minimum(to * width, model - width), LANES)
+        copies.append(
+            pltpu.make_async_copy(down_ref.at[:, pl.ds(start, width)], block_ref, sems.at[at])
+        )
     run(copies)
 
 
@@ -150,19 +144,25 @@
     out_ref[...] = (gate * jax.nn.sigmoid(gate) * up).astype(jnp.bfloat16)
 
 
-def down_kernel(hidden_ref, kept_ref, next_ref, last_ref, out_ref):
-    slots = hidden_ref.shape[1]
+def down_kernel(hidden_ref, next_ref, last_ref, kept_ref, mine_ref, sent_ref):
+    width = mine_ref.shape[1]
+    third, core = lax.axis_index("j"), lax.axis_index("k")
+    for out_ref, who in ((sent_ref, 1 - core), (mine_ref, core)):
+        columns = pl.ds(pl.multiple_of(who * width, LANES), width)
+        total = None
+        for step, weights_ref in ((0, kept_ref), (1, next_ref), (2, last_ref)):
+            source = lax.rem(third + 3 - step, 3)
+            term = dot(hidden_ref[source], weights_ref[:, columns])
+            total = term if total is None else total + term
+        out_ref[...] = total.astype(out_ref.dtype)
+
+
+def pack_kernel(mine_ref, sent_ref, out_ref):
+    slots, columns = mine_ref.shape
     rows, width = out_ref.shape
-    columns = next_ref.shape[2]
-    third, core = lax.axis_index("j"), lax.axis_index("k")
-    total = None
-    for step, weights in enumerate((kept_ref, next_ref, last_ref)):
-        source = lax.rem(third + 3 - step, 3)
-        for which in range(CORES):
-            who = core if which == 0 else 1 - core
-            term = dot(hidden_ref[CORES * source + who], weights[which])
-            total = term if total is None else total + term
-    piece = total.astype(jnp.bfloat16)
+    piece = (mine_ref[...] + sent_ref[1 - lax.axis_index("k")].astype(jnp.float32)).astype(
+        jnp.bfloat16
+    )
     out = None
     row, slot = iota((rows, slots), 0), iota((rows, slots), 1)
     hit = slot == (row >> 4) * CAP + (row & 3)
@@ -205,13 +205,11 @@
     total = parts[:per_group]
     for group in range(1, EXP_DP):
         total = total + parts[group * per_group : (group + 1) * per_group]
-    half = model // CORES
     for part in range(per_group // rows):
         third, core = part // CORES, part % CORES
-        base = min(third * width, half - width)
-        skip = third * width - base
+        base = min(third * CORES * width, model - CORES * width) + core * width
+        skip = max(0, part * width - base) if core == 0 else 0
         block = total[part * rows : (part + 1) * rows, skip:] * gates
-        base += core * half
         out_ref[:, base + skip : base + width] = block.astype(jnp.bfloat16)
 
 
@@ -263,25 +261,17 @@
         (in_hbm(routes_row), in_hbm(tokens)),
         scratch_shapes=[
             pltpu.VMEM((1, tok_rows), jnp.int32),
-            pltpu.VMEM((QUARTERS, tok_rows, half // QUARTERS), bf),
-            pltpu.SemaphoreType.DMA((QUARTERS + 1,)),
+            pltpu.VMEM((tok_rows, half), bf),
+            pltpu.SemaphoreType.DMA((3,)),
         ],
     )
     arrived = over_dp(outgoing.reshape(dp_count, CHUNK, half // QUARTERS))
-    away = call(
-        away_kernel,
-        array((units, half)),
+    *sent, kept = call(
+        blocks_kernel,
+        [array((units, CORES * width))] * thirds,
         [HBM],
         (w_down,),
-        scratch_shapes=[pltpu.SemaphoreType.DMA],
-    )
-    given = exchange(away)
-    kept, *sent = call(
-        blocks_kernel,
-        [pltpu.HBM((CORES, units, width), bf)] + [array((CORES, units, width))] * (thirds - 1),
-        [HBM, HBM],
-        (w_down, given),
-        scratch_shapes=[pltpu.SemaphoreType.DMA((CORES * thirds,))],
+        scratch_shapes=[pltpu.SemaphoreType.DMA((thirds,))],
     )
     arrived = lax.optimization_barrier((arrived, sent))[0]
     moved = [
@@ -315,12 +305,18 @@
         [VMEM] * 3,
         (partial, other.reshape(flat), joined(False, partial)),
     )
-    all_hidden = lax.all_gather(hidden, ("j", "k"), axis=0)
+    all_hidden = lax.all_gather(hidden, "j", axis=0)
+    mine, others = call(
+        down_kernel,
+        [array((slots, width), f32), array((slots, width))],
+        [VMEM] * (1 + thirds),
+        (all_hidden, *moved, kept),
+    )
     piece = call(
-        down_kernel,
+        pack_kernel,
         array((dp_count * CHUNK, quarter)),
-        [VMEM] * (1 + thirds),
-        (all_hidden, kept, *moved),
+        [VMEM] * 2,
+        (mine, lax.all_gather(others, "k", axis=0)),
     )
     back = over_dp(piece.reshape(dp_count, CHUNK, quarter))
     spread = call(

time: 110 us -> 106 us (0.964)
  blocking collectives: 67.7 us -> 64.4 us
  waiting for transfers between devices: 6.37 us -> 8.41 us
  starting transfers between devices: 23.7 us -> 21.8 us
    all_to_all x1, blocking collectives: 22.2 us -> 17.4 us  [over_dp(): return lax.all_to_all(x, 'dp', split_axis=0, concat_axis=0, tiled=True)]
    all_to_all x1, waiting for transfers between devices: 4.29 us -> 8.4 us  [over_dp(): return lax.all_to_all(x, 'dp', split_axis=0, concat_axis=0, tiled=True)]
    ppermute x2 -> x1, waiting for transfers between devices: 2.07 us -> 0.01 us  [exchange(): return lax.ppermute(x, 'k', [(0, 1), (1, 0)])]
    ppermute x2 -> x1, starting transfers between devices: 3.83 us -> 1.91 us  [exchange(): return lax.ppermute(x, 'k', [(0, 1), (1, 0)])]
    all_gather x1 -> x2, blocking collectives: 11.8 us -> 13.1 us  [the longest x1 11 us: per_device(): all_hidden = lax.all_gather(hidden, 'j', axis=0)]
  transfers between devices with their start and end apart: 5 -> 4, of which waited for: 2 -> 1; matrix products, arithmetic and copies ran while one was open for 0% -> 0% of each run, Pallas kernels for 5% -> 5%
where the time goes in v3:
time: 106 us
  blocking collectives  64.4 us (61%)
  starting transfers between devices  21.8 us (21%)
  Pallas kernels  11 us (10%)
  waiting for transfers between devices  8.41 us (8%)
    all_to_all x1, blocking collectives, per_device(): lax.all_to_all(spread.reshape(owners, tok_rows // owners, width), ('g', '...  33.8 us
    all_to_all x1, blocking collectives, over_dp(): return lax.all_to_all(x, 'dp', split_axis=0, concat_axis=0, tiled=True)  17.4 us
    all_to_all x1, starting transfers between devices, over_dp(): return lax.all_to_all(x, 'dp', split_axis=0, concat_axis=0, tiled=True)  13.2 us
    pallas_call x10, Pallas kernels, call(): pl.pallas_call(kernel, out_shape=shapes, in_specs=in_specs, out_specs=VME...  11 us
    all_gather x1, blocking collectives, per_device(): all_hidden = lax.all_gather(hidden, 'j', axis=0)  11 us
    all_to_all x1, waiting for transfers between devices, over_dp(): return lax.all_to_all(x, 'dp', split_axis=0, concat_axis=0, tiled=True)  8.4 us
    ppermute x2, starting transfers between devices, per_device(): lax.ppermute(block, 'j', [(i, (i + step) % thirds) for i in range(thirds)])  6.74 us
    all_gather x1, blocking collectives, per_device(): lax.all_gather(others, 'k', axis=0)  2.14 us
  transfers between devices with their start and end apart: 4, of which 1 were waited for; matrix products, arithmetic and copies ran while one was open for 0% of the time, Pallas kernels for 5%

profile of v3, /device:TPU:8, one launch (start us, length us, event | category | flops | bytes accessed | tf_op | source)
XLA Modules:
  0.0 105.7 jit_solution(11182333159257913461)
XLA Ops:
  0.0 3.0 %shard_map.64 = bf16[512,640]{1,0:T(8,128)(2,1)} custom-call(s32[1,192]{1,0:T(1,128)} %bitcast.20, bf16[192,5120]{1,0:T(8,128)(2,1)} %tokens_ref.1), custom_call_target="tpu_custom_call" | custom-call | tf_op jit(solution)/shard_map/pallas_call | solution.py:218
  3.0 0.0 copy-start
  3.1 13.2 %all-to-all-start = ((bf16[32,16,640]{2,1,0:T(8,128)(2,1)}), bf16[32,16,640]{2,1,0:T(8,128)(2,1)S(1)}, u32[]{:S(2)}, u32[]{:S(2)}) async-start(bf16[32,16,640]{2,1,0:T(8,128)(2,1)} %bitcast.2), calls=%async_computation | async-start | bytes 1310720 | tf_op jit(solution)/shard_map/all_to_all | solution.py:237
  16.2 0.0 copy-done
  16.2 1.1 %shard_map.65 = (bf16[128,1792]{1,0:T(8,128)(2,1)}, bf16[128,1792]{1,0:T(8,128)(2,1)}, bf16[128,1792]{1,0:T(8,128)(2,1)S(1)}) custom-call(bf16[128,5120]{1,0:T(8,128)(2,1)S(1)} %copy-done), custom_call_target="tpu_custom_call" | custom-call | tf_op jit(solution)/shard_map/pallas_call | solution.py:218
  17.4 1.9 %collective-permute-start.1 = (bf16[128,1792]{1,0:T(8,128)(2,1)}, bf16[128,1792]{1,0:T(8,128)(2,1)S(1)}, u32[]{:S(2)}, u32[]{:S(2)}) collective-permute-start(bf16[128,1792]{1,0:T(8,128)(2,1)} %get-tuple-element.15), channel_id=1, source_target_pairs={{0,2},{2,4},{4,0},{1,3},{3,5},{5,1},{6,8},{8,10},{10,6},{7,9},{9,1... | collective-permute-start | bytes 1376264 | tf_op jit(solution)/shard_map/ppermute | solution.py:278
  19.3 4.8 %collective-permute-start.2 = (bf16[128,1792]{1,0:T(8,128)(2,1)}, bf16[128,1792]{1,0:T(8,128)(2,1)S(1)}, u32[]{:S(2)}, u32[]{:S(2)}) collective-permute-start(bf16[128,1792]{1,0:T(8,128)(2,1)} %get-tuple-element.16), channel_id=1, source_target_pairs={{0,4},{2,0},{4,2},{1,5},{3,1},{5,3},{6,10},{8,6},{10,8},{7,11},{9,... | collective-permute-start | bytes 1376264 | tf_op jit(solution)/shard_map/ppermute | solution.py:278
  24.1 1.3 %shard_map.66.weights_ref = bf16[2560,256]{1,0:T(8,128)(2,1)S(1)} custom-call(bf16[5120,128]{1,0:T(8,128)(2,1)} %gate_ref.1, bf16[5120,128]{1,0:T(8,128)(2,1)} %up_ref.1), custom_call_target="tpu_custom_call" | custom-call | tf_op jit(solution)/shard_map/pallas_call | solution.py:218
  25.5 8.4 %all-to-all-done = bf16[32,16,640]{2,1,0:T(8,128)(2,1)S(1)} async-done(((bf16[32,16,640]{2,1,0:T(8,128)(2,1)}), bf16[32,16,640]{2,1,0:T(8,128)(2,1)S(1)}, u32[]{:S(2)}, u32[]{:S(2)}) %all-to-all-start) | async-done | bytes 655392 | tf_op jit(solution)/shard_map/all_to_all | solution.py:237
  33.9 1.9 %collective-permute-start = (bf16[32,16,640]{2,1,0:T(8,128)(2,1)S(1)}, bf16[32,16,640]{2,1,0:T(8,128)(2,1)S(1)}, u32[]{:S(2)}, u32[]{:S(2)}) collective-permute-start(bf16[32,16,640]{2,1,0:T(8,128)(2,1)S(1)} %all-to-all-done), channel_id=1, source_target_pairs={{0,1},{1,0},{2,3},{3,2},{4,5},{5,4},{6,7},{7,6},{8,9},{9,8},{10,11... | collective-permute-start | bytes 1966088 | tf_op jit(solution)/shard_map/ppermute | solution.py:233
  35.8 0.9 shard_map.67.partial_ref
  36.7 1.3 %shard_map.68.weights_ref = bf16[2560,256]{1,0:T(8,128)(2,1)S(1)} custom-call(bf16[5120,128]{1,0:T(8,128)(2,1)} %gate_ref.1, bf16[5120,128]{1,0:T(8,128)(2,1)} %up_ref.1), custom_call_target="tpu_custom_call" | custom-call | flops 8000000000 | bytes 16777216 | tf_op jit(solution)/shard_map/pallas_call | solution.py:218
  38.0 0.0 collective-permute-done
  38.1 1.0 shard_map.69
  39.0 11.0 %all-gather = bf16[384,128]{1,0:T(8,128)(2,1)S(1)} all-gather(bf16[128,128]{1,0:T(8,128)(2,1)S(1)} %shard_map.69), channel_id=2, replica_groups=mesh['dp'=32,'g'=4,'j'=3,'k'=2] {'j'}, dimensions={0}, use_global_device_ids=true | all-gather | bytes 131072 | tf_op jit(solution)/shard_map/all_gather | solution.py:308
  50.0 0.0 collective-permute-done.1.next_ref
  50.0 0.0 collective-permute-done.2.last_ref
  50.0 0.5 shard_map.70
  50.5 0.0 copy-start.2
  50.6 2.1 %all-gather.1 = bf16[256,896]{1,0:T(8,128)(2,1)S(1)} all-gather(bf16[128,896]{1,0:T(8,128)(2,1)S(1)} %get-tuple-element.24), channel_id=3, replica_groups=mesh['dp'=32,'g'=4,'j'=3,'k'=2] {'k'}, dimensions={0}, use_global_device_ids=true | all-gather | bytes 688128 | tf_op jit(solution)/shard_map/all_gather | solution.py:319
  52.7 0.0 copy-start.1
  52.7 0.4 shard_map.71
  53.1 17.4 %all_to_all.15 = bf16[32,16,256]{2,1,0:T(8,128)(2,1)S(1)} all-to-all(bf16[32,16,256]{2,1,0:T(8,128)(2,1)S(1)} %bitcast.15), channel_id=1, replica_groups=mesh['dp'=32,'g'=4,'j'=3,'k'=2] {'dp'}, dimensions={0} | all-to-all | bytes 524288 | tf_op jit(solution)/shard_map/all_to_all | solution.py:237
  70.5 0.0 copy-done.2
  70.5 0.6 shard_map.72
  71.2 33.8 %all_to_all.16 = bf16[24,8,896]{2,1,0:T(8,128)(2,1)S(1)} all-to-all(bf16[24,8,896]{2,1,0:T(8,128)(2,1)S(1)} %bitcast.12), channel_id=1, replica_groups=mesh['dp'=32,'g'=4,'j'=3,'k'=2] {'g','j','k'}, dimensions={0} | all-to-all | bytes 688128 | tf_op jit(solution)/shard_map/all_to_all | solution.py:328
  105.0 0.0 copy-done.1
  105.0 0.7 shard_map.73
Async XLA Ops:
  3.0 13.2 %copy-start = (bf16[128,5120]{1,0:T(8,128)(2,1)S(1)}, bf16[128,5120]{1,0:T(8,128)(2,1)}, u32[]{:S(2)}) copy-start(bf16[128,5120]{1,0:T(8,128)(2,1)} %down_ref.1) | copy-start | bytes 3932164
  3.1 30.8 %all-to-all-start = ((bf16[32,16,640]{2,1,0:T(8,128)(2,1)}), bf16[32,16,640]{2,1,0:T(8,128)(2,1)S(1)}, u32[]{:S(2)}, u32[]{:S(2)}) async-start(bf16[32,16,640]{2,1,0:T(8,128)(2,1)} %bitcast.2), calls=%async_computation | async-start | bytes 1310720 | tf_op jit(solution)/shard_map/all_to_all | solution.py:237
  17.4 32.6 %collective-permute-start.1 = (bf16[128,1792]{1,0:T(8,128)(2,1)}, bf16[128,1792]{1,0:T(8,128)(2,1)S(1)}, u32[]{:S(2)}, u32[]{:S(2)}) collective-permute-start(bf16[128,1792]{1,0:T(8,128)(2,1)} %get-tuple-element.15), channel_id=1, source_target_pairs={{0,2},{2,4},{4,0},{1,3},{3,5},{5,1},{6,8},{8,10},{10,6},{7,9},{9,1... | collective-permute-start | bytes 1376264 | tf_op jit(solution)/shard_map/ppermute | solution.py:278
  19.3 30.7 %collective-permute-start.2 = (bf16[128,1792]{1,0:T(8,128)(2,1)}, bf16[128,1792]{1,0:T(8,128)(2,1)S(1)}, u32[]{:S(2)}, u32[]{:S(2)}) collective-permute-start(bf16[128,1792]{1,0:T(8,128)(2,1)} %get-tuple-element.16), channel_id=1, source_target_pairs={{0,4},{2,0},{4,2},{1,5},{3,1},{5,3},{6,10},{8,6},{10,8},{7,11},{9,... | collective-permute-start | bytes 1376264 | tf_op jit(solution)/shard_map/ppermute | solution.py:278
  33.9 4.2 %collective-permute-start = (bf16[32,16,640]{2,1,0:T(8,128)(2,1)S(1)}, bf16[32,16,640]{2,1,0:T(8,128)(2,1)S(1)}, u32[]{:S(2)}, u32[]{:S(2)}) collective-permute-start(bf16[32,16,640]{2,1,0:T(8,128)(2,1)S(1)} %all-to-all-done), channel_id=1, source_target_pairs={{0,1},{1,0},{2,3},{3,2},{4,5},{5,4},{6,7},{7,6},{8,9},{9,8},{10,11... | collective-permute-start | bytes 1966088 | tf_op jit(solution)/shard_map/ppermute | solution.py:233
  50.5 20.0 %copy-start.2 = (s32[192,1]{0,1:T(1,128)S(1)}, s32[192,1]{0,1:T(1,128)}, u32[]{:S(2)}) copy-start(s32[192,1]{0,1:T(1,128)} %param.8) | copy-start | bytes 2308
  52.7 52.3 %copy-start.1 = (f32[192,8]{0,1:T(8,128)S(1)}, f32[192,8]{0,1:T(8,128)}, u32[]{:S(2)}) copy-start(f32[192,8]{0,1:T(8,128)} %param.7) | copy-start | bytes 18436

commit v4 on v3

--- a/solution.py
+++ b/solution.py
@@ -177,11 +177,22 @@
     out_ref[...] = out.astype(jnp.bfloat16)
 
 
-def spread_kernel(routes_ref, back_ref, out_ref):
+def ahead_kernel(routes_ref, scores_ref, first_ref, gates_ref):
+    slot = slots_of_tokens(routes_ref[...], lax.axis_index("g"), True)
+    first_ref[...] = (slot >> 2) * CHUNK + (slot & 3)
+    rows, tokens = gates_ref.shape[0], scores_ref.shape[1]
+    sig = jax.nn.sigmoid(scores_ref[...])
+    gates = ROUTE_SCALE * sig[:1] / jnp.sum(sig, axis=0, keepdims=True)
+    owner = (lax.axis_index("g") * lax.axis_size("j") + lax.axis_index("j")) * CORES
+    owner += lax.axis_index("k")
+    mine = iota((rows, tokens), 1) == owner * rows + iota((rows, tokens), 0)
+    gates_ref[...] = jnp.sum(jnp.where(mine, gates, 0.0), axis=1, keepdims=True)
+
+
+def spread_kernel(first_ref, back_ref, out_ref):
     rows, width = back_ref.shape
     tokens, columns = out_ref.shape
-    slot = slots_of_tokens(routes_ref[...], lax.axis_index("g"), True)
-    first = (slot >> 2) * CHUNK + (slot & 3)
+    first = first_ref[...]
     row = iota((tokens, rows), 1)
     back = back_ref[...]
     for q in range(QUARTERS):
@@ -190,16 +201,10 @@
         out_ref[:, q * width : stop] = block.astype(jnp.bfloat16)
 
 
-def finish_kernel(scores_ref, parts_ref, out_ref):
+def finish_kernel(gates_ref, parts_ref, out_ref):
     rows, model = out_ref.shape
     width = parts_ref.shape[1]
-    tokens = scores_ref.shape[1]
-    sig = jax.nn.sigmoid(scores_ref[...])
-    gates = ROUTE_SCALE * sig[:1] / jnp.sum(sig, axis=0, keepdims=True)
-    owner = (lax.axis_index("g") * lax.axis_size("j") + lax.axis_index("j")) * CORES
-    owner += lax.axis_index("k")
-    mine = iota((rows, tokens), 1) == owner * rows + iota((rows, tokens), 0)
-    gates = jnp.sum(jnp.where(mine, gates, 0.0), axis=1, keepdims=True)
+    gates = gates_ref[...]
     parts = parts_ref[...].astype(jnp.float32)
     per_group = parts.shape[0] // EXP_DP
     total = parts[:per_group]
@@ -273,7 +278,13 @@
         (w_down,),
         scratch_shapes=[pltpu.SemaphoreType.DMA((thirds,))],
     )
-    arrived = lax.optimization_barrier((arrived, sent))[0]
+    first, gates = call(
+        ahead_kernel,
+        [array((tok_rows, 1), jnp.int32), array((tok_rows // owners, 1), f32)],
+        [VMEM] * 2,
+        lax.optimization_barrier((routes_row, scores_row, sent))[:2],
+    )
+    arrived = lax.optimization_barrier((arrived, sent, first, gates))[0]
     moved = [
         lax.ppermute(block, "j", [(i, (i + step) % thirds) for i in range(thirds)])
         for step, block in enumerate(sent, 1)
@@ -323,7 +334,7 @@
         spread_kernel,
         array((tok_rows, width)),
         [VMEM, VMEM],
-        (routes_row, back.reshape(dp_count * CHUNK, quarter)),
+        (first, back.reshape(dp_count * CHUNK, quarter)),
     )
     final = lax.all_to_all(
         spread.reshape(owners, tok_rows // owners, width),
@@ -336,7 +347,7 @@
         finish_kernel,
         array((tok_rows // owners, model)),
         [VMEM, VMEM],
-        (scores_row, final.reshape(tok_rows, width)),
+        (gates, final.reshape(tok_rows, width)),
     )
 
 

time: 106 us -> 106 us (level)
    pallas_call x10 -> x11, Pallas kernels: 11 us -> 11 us  [call(): pl.pallas_call(kernel, out_shape=shapes, in_specs=in_specs, out_specs=VME...]
  transfers between devices with their start and end apart: 4 -> 4, of which waited for: 1 -> 1; matrix products, arithmetic and copies ran while one was open for 0% -> 0% of each run, Pallas kernels for 5% -> 6%
where the time goes in v4:
time: 106 us
  blocking collectives  64.4 us (61%)
  starting transfers between devices  21.8 us (21%)
  Pallas kernels  11 us (10%)
  waiting for transfers between devices  8.13 us (8%)
    all_to_all x1, blocking collectives, per_device(): lax.all_to_all(spread.reshape(owners, tok_rows // owners, width), ('g', '...  33.8 us
    all_to_all x1, blocking collectives, over_dp(): return lax.all_to_all(x, 'dp', split_axis=0, concat_axis=0, tiled=True)  17.4 us
    all_to_all x1, starting transfers between devices, over_dp(): return lax.all_to_all(x, 'dp', split_axis=0, concat_axis=0, tiled=True)  13.2 us
    pallas_call x11, Pallas kernels, call(): pl.pallas_call(kernel, out_shape=shapes, in_specs=in_specs, out_specs=VME...  11 us
    all_gather x1, blocking collectives, per_device(): all_hidden = lax.all_gather(hidden, 'j', axis=0)  11 us
    all_to_all x1, waiting for transfers between devices, over_dp(): return lax.all_to_all(x, 'dp', split_axis=0, concat_axis=0, tiled=True)  8.12 us
    ppermute x2, starting transfers between devices, per_device(): lax.ppermute(block, 'j', [(i, (i + step) % thirds) for i in range(thirds)])  6.74 us
    all_gather x1, blocking collectives, per_device(): lax.all_gather(others, 'k', axis=0)  2.14 us
  transfers between devices with their start and end apart: 4, of which 1 were waited for; matrix products, arithmetic and copies ran while one was open for 0% of the time, Pallas kernels for 6%

profile of v4, /device:TPU:8, one launch (start us, length us, event | category | flops | bytes accessed | tf_op | source)
XLA Modules:
  0.0 105.5 jit_solution(2531677607832161573)
XLA Ops:
  0.0 3.0 %shard_map.66 = bf16[512,640]{1,0:T(8,128)(2,1)} custom-call(s32[1,192]{1,0:T(1,128)} %bitcast.20, bf16[192,5120]{1,0:T(8,128)(2,1)} %tokens_ref.1), custom_call_target="tpu_custom_call" | custom-call | tf_op jit(solution)/shard_map/pallas_call | solution.py:223
  3.1 0.0 copy-start
  3.1 0.0 copy-start.1
  3.1 0.0 copy-start.2
  3.1 13.2 %all-to-all-start = ((bf16[32,16,640]{2,1,0:T(8,128)(2,1)}), bf16[32,16,640]{2,1,0:T(8,128)(2,1)S(1)}, u32[]{:S(2)}, u32[]{:S(2)}) async-start(bf16[32,16,640]{2,1,0:T(8,128)(2,1)} %bitcast.2), calls=%async_computation | async-start | bytes 1310720 | tf_op jit(solution)/shard_map/all_to_all | solution.py:242
  16.3 0.0 copy-done
  16.3 1.2 %shard_map.64 = (bf16[128,1792]{1,0:T(8,128)(2,1)}, bf16[128,1792]{1,0:T(8,128)(2,1)}, bf16[128,1792]{1,0:T(8,128)(2,1)S(1)}) custom-call(bf16[128,5120]{1,0:T(8,128)(2,1)S(1)} %copy-done), custom_call_target="tpu_custom_call" | custom-call | tf_op jit(solution)/shard_map/pallas_call | solution.py:223
  17.4 1.9 %collective-permute-start.1 = (bf16[128,1792]{1,0:T(8,128)(2,1)}, bf16[128,1792]{1,0:T(8,128)(2,1)S(1)}, u32[]{:S(2)}, u32[]{:S(2)}) collective-permute-start(bf16[128,1792]{1,0:T(8,128)(2,1)} %get-tuple-element.19), channel_id=1, source_target_pairs={{0,2},{2,4},{4,0},{1,3},{3,5},{5,1},{6,8},{8,10},{10,6},{7,9},{9,1... | collective-permute-start | bytes 1376264 | tf_op jit(solution)/shard_map/ppermute | solution.py:289
  19.4 4.8 %collective-permute-start.2 = (bf16[128,1792]{1,0:T(8,128)(2,1)}, bf16[128,1792]{1,0:T(8,128)(2,1)S(1)}, u32[]{:S(2)}, u32[]{:S(2)}) collective-permute-start(bf16[128,1792]{1,0:T(8,128)(2,1)} %get-tuple-element.20), channel_id=1, source_target_pairs={{0,4},{2,0},{4,2},{1,5},{3,1},{5,3},{6,10},{8,6},{10,8},{7,11},{9,... | collective-permute-start | bytes 1376264 | tf_op jit(solution)/shard_map/ppermute | solution.py:289
  24.2 0.0 copy-done.1
  24.2 0.0 copy-done.2
  24.2 0.2 shard_map.65
  24.5 1.3 %shard_map.67.weights_ref = bf16[2560,256]{1,0:T(8,128)(2,1)S(1)} custom-call(bf16[5120,128]{1,0:T(8,128)(2,1)} %gate_ref.1, bf16[5120,128]{1,0:T(8,128)(2,1)} %up_ref.1), custom_call_target="tpu_custom_call" | custom-call | tf_op jit(solution)/shard_map/pallas_call | solution.py:223
  25.8 8.1 %all-to-all-done = bf16[32,16,640]{2,1,0:T(8,128)(2,1)S(1)} async-done(((bf16[32,16,640]{2,1,0:T(8,128)(2,1)}), bf16[32,16,640]{2,1,0:T(8,128)(2,1)S(1)}, u32[]{:S(2)}, u32[]{:S(2)}) %all-to-all-start) | async-done | bytes 655392 | tf_op jit(solution)/shard_map/all_to_all | solution.py:242
  33.9 1.9 %collective-permute-start = (bf16[32,16,640]{2,1,0:T(8,128)(2,1)S(1)}, bf16[32,16,640]{2,1,0:T(8,128)(2,1)S(1)}, u32[]{:S(2)}, u32[]{:S(2)}) collective-permute-start(bf16[32,16,640]{2,1,0:T(8,128)(2,1)S(1)} %all-to-all-done), channel_id=1, source_target_pairs={{0,1},{1,0},{2,3},{3,2},{4,5},{5,4},{6,7},{7,6},{8,9},{9,8},{10,11... | collective-permute-start | bytes 1966088 | tf_op jit(solution)/shard_map/ppermute | solution.py:238
  35.8 0.9 shard_map.68.partial_ref
  36.8 1.3 %shard_map.69.weights_ref = bf16[2560,256]{1,0:T(8,128)(2,1)S(1)} custom-call(bf16[5120,128]{1,0:T(8,128)(2,1)} %gate_ref.1, bf16[5120,128]{1,0:T(8,128)(2,1)} %up_ref.1), custom_call_target="tpu_custom_call" | custom-call | flops 8000000000 | bytes 16777216 | tf_op jit(solution)/shard_map/pallas_call | solution.py:223
  38.1 0.0 collective-permute-done
  38.1 1.0 shard_map.70
  39.1 11.0 %all-gather = bf16[384,128]{1,0:T(8,128)(2,1)S(1)} all-gather(bf16[128,128]{1,0:T(8,128)(2,1)S(1)} %shard_map.70), channel_id=2, replica_groups=mesh['dp'=32,'g'=4,'j'=3,'k'=2] {'j'}, dimensions={0}, use_global_device_ids=true | all-gather | bytes 131072 | tf_op jit(solution)/shard_map/all_gather | solution.py:319
  50.0 0.0 collective-permute-done.1.next_ref
  50.0 0.0 collective-permute-done.2.last_ref
  50.1 0.5 shard_map.71
  50.6 2.1 %all-gather.1 = bf16[256,896]{1,0:T(8,128)(2,1)S(1)} all-gather(bf16[128,896]{1,0:T(8,128)(2,1)S(1)} %get-tuple-element.32), channel_id=3, replica_groups=mesh['dp'=32,'g'=4,'j'=3,'k'=2] {'k'}, dimensions={0}, use_global_device_ids=true | all-gather | bytes 688128 | tf_op jit(solution)/shard_map/all_gather | solution.py:330
  52.7 0.4 shard_map.72
  53.1 17.4 %all_to_all.15 = bf16[32,16,256]{2,1,0:T(8,128)(2,1)S(1)} all-to-all(bf16[32,16,256]{2,1,0:T(8,128)(2,1)S(1)} %bitcast.14), channel_id=1, replica_groups=mesh['dp'=32,'g'=4,'j'=3,'k'=2] {'dp'}, dimensions={0} | all-to-all | bytes 524288 | tf_op jit(solution)/shard_map/all_to_all | solution.py:242
  70.5 0.4 shard_map.73
  71.0 33.8 %all_to_all.16 = bf16[24,8,896]{2,1,0:T(8,128)(2,1)S(1)} all-to-all(bf16[24,8,896]{2,1,0:T(8,128)(2,1)S(1)} %bitcast.12), channel_id=1, replica_groups=mesh['dp'=32,'g'=4,'j'=3,'k'=2] {'g','j','k'}, dimensions={0} | all-to-all | bytes 688128 | tf_op jit(solution)/shard_map/all_to_all | solution.py:339
  104.8 0.7 shard_map.74
Async XLA Ops:
  3.1 13.2 %copy-start = (bf16[128,5120]{1,0:T(8,128)(2,1)S(1)}, bf16[128,5120]{1,0:T(8,128)(2,1)}, u32[]{:S(2)}) copy-start(bf16[128,5120]{1,0:T(8,128)(2,1)} %down_ref.1) | copy-start | bytes 3932164
  3.1 21.1 %copy-start.1 = (f32[192,8]{0,1:T(8,128)S(1)}, f32[192,8]{0,1:T(8,128)}, u32[]{:S(2)}) copy-start(f32[192,8]{0,1:T(8,128)} %param.7) | copy-start | bytes 18436
  3.1 21.1 %copy-start.2 = (s32[192,1]{0,1:T(1,128)S(1)}, s32[192,1]{0,1:T(1,128)}, u32[]{:S(2)}) copy-start(s32[192,1]{0,1:T(1,128)} %param.8) | copy-start | bytes 2308
  3.1 30.8 %all-to-all-start = ((bf16[32,16,640]{2,1,0:T(8,128)(2,1)}), bf16[32,16,640]{2,1,0:T(8,128)(2,1)S(1)}, u32[]{:S(2)}, u32[]{:S(2)}) async-start(bf16[32,16,640]{2,1,0:T(8,128)(2,1)} %bitcast.2), calls=%async_computation | async-start | bytes 1310720 | tf_op jit(solution)/shard_map/all_to_all | solution.py:242
  17.4 32.6 %collective-permute-start.1 = (bf16[128,1792]{1,0:T(8,128)(2,1)}, bf16[128,1792]{1,0:T(8,128)(2,1)S(1)}, u32[]{:S(2)}, u32[]{:S(2)}) collective-permute-start(bf16[128,1792]{1,0:T(8,128)(2,1)} %get-tuple-element.19), channel_id=1, source_target_pairs={{0,2},{2,4},{4,0},{1,3},{3,5},{5,1},{6,8},{8,10},{10,6},{7,9},{9,1... | collective-permute-start | bytes 1376264 | tf_op jit(solution)/shard_map/ppermute | solution.py:289
  19.4 30.7 %collective-permute-start.2 = (bf16[128,1792]{1,0:T(8,128)(2,1)}, bf16[128,1792]{1,0:T(8,128)(2,1)S(1)}, u32[]{:S(2)}, u32[]{:S(2)}) collective-permute-start(bf16[128,1792]{1,0:T(8,128)(2,1)} %get-tuple-element.20), channel_id=1, source_target_pairs={{0,4},{2,0},{4,2},{1,5},{3,1},{5,3},{6,10},{8,6},{10,8},{7,11},{9,... | collective-permute-start | bytes 1376264 | tf_op jit(solution)/shard_map/ppermute | solution.py:289
  33.9 4.2 %collective-permute-start = (bf16[32,16,640]{2,1,0:T(8,128)(2,1)S(1)}, bf16[32,16,640]{2,1,0:T(8,128)(2,1)S(1)}, u32[]{:S(2)}, u32[]{:S(2)}) collective-permute-start(bf16[32,16,640]{2,1,0:T(8,128)(2,1)S(1)} %all-to-all-done), channel_id=1, source_target_pairs={{0,1},{1,0},{2,3},{3,2},{4,5},{5,4},{6,7},{7,6},{8,9},{9,8},{10,11... | collective-permute-start | bytes 1966088 | tf_op jit(solution)/shard_map/ppermute | solution.py:238

commit v5 on v4

--- a/solution.py
+++ b/solution.py
@@ -1,5 +1,3 @@
-import functools
-
 import jax
 import jax.numpy as jnp
 from jax import lax
@@ -103,18 +101,8 @@
     run(copies)
 
 
-def join_kernel(own, gate_ref, up_ref, out_ref, sems):
-    half, units = out_ref.shape[0], gate_ref.shape[1]
-    me = lax.axis_index("k")
-    start = pl.multiple_of((me if own else 1 - me) * half, LANES)
-    run(
-        [
-            pltpu.make_async_copy(
-                w_ref.at[pl.ds(start, half)], out_ref.at[:, pl.ds(at * units, units)], sems.at[at]
-            )
-            for at, w_ref in enumerate((gate_ref, up_ref))
-        ]
-    )
+def stage_kernel(from_ref, out_ref, sem):
+    run([pltpu.make_async_copy(from_ref, out_ref, sem)])
 
 
 def unpack(slots, rows, q):
@@ -122,25 +110,30 @@
     return one_hot(row == (slot >> 2) * CHUNK + q * CAP + (slot & 3))
 
 
-def project(chunks_ref, weights_ref, slots):
+def project(core, chunks_ref, gate_ref, up_ref, slots):
     rows, width = chunks_ref.shape
     chunks = chunks_ref[...]
-    total = None
+    totals = [None, None]
     for q in range(QUARTERS):
         part = dot(unpack(slots, rows, q), chunks).astype(jnp.bfloat16)
-        term = dot(part, weights_ref[q * width : (q + 1) * width, :])
-        total = term if total is None else total + term
-    return total
-
-
-def own_kernel(chunks_ref, weights_ref, out_ref):
-    out_ref[...] = project(chunks_ref, weights_ref, out_ref.shape[0])
-
-
-def hidden_kernel(partial_ref, chunks_ref, weights_ref, out_ref):
-    slots, units = out_ref.shape
-    pre = partial_ref[...] + project(chunks_ref, weights_ref, slots)
-    gate, up = pre[:, :units], pre[:, units:]
+        columns = pl.ds(pl.multiple_of((core * QUARTERS + q) * width, LANES), width)
+        for at, weights_ref in enumerate((gate_ref, up_ref)):
+            term = dot(part, weights_ref[columns, :])
+            totals[at] = term if totals[at] is None else totals[at] + term
+    return totals
+
+
+def own_kernel(chunks_ref, gate_ref, up_ref, pre_gate_ref, pre_up_ref):
+    pre_gate_ref[...], pre_up_ref[...] = project(
+        lax.axis_index("k"), chunks_ref, gate_ref, up_ref, pre_up_ref.shape[0]
+    )
+
+
+def hidden_kernel(pre_gate_ref, pre_up_ref, chunks_ref, gate_ref, up_ref, out_ref):
+    core = 1 - lax.axis_index("k")
+    gate, up = project(core, chunks_ref, gate_ref, up_ref, out_ref.shape[0])
+    gate += pre_gate_ref[...]
+    up += pre_up_ref[...]
     out_ref[...] = (gate * jax.nn.sigmoid(gate) * up).astype(jnp.bfloat16)
 
 
@@ -273,7 +266,7 @@
     arrived = over_dp(outgoing.reshape(dp_count, CHUNK, half // QUARTERS))
     *sent, kept = call(
         blocks_kernel,
-        [array((units, CORES * width))] * thirds,
+        [array((units, CORES * width))] * (thirds - 1) + [pltpu.HBM((units, CORES * width), bf)],
         [HBM],
         (w_down,),
         scratch_shapes=[pltpu.SemaphoreType.DMA((thirds,))],
@@ -283,6 +276,13 @@
         [array((tok_rows, 1), jnp.int32), array((tok_rows // owners, 1), f32)],
         [VMEM] * 2,
         lax.optimization_barrier((routes_row, scores_row, sent))[:2],
+    )
+    w_up = call(
+        stage_kernel,
+        pltpu.VMEM(w_up.shape, bf),
+        [HBM],
+        (in_hbm(lax.optimization_barrier((w_up, sent))[0]),),
+        scratch_shapes=[pltpu.SemaphoreType.DMA],
     )
     arrived = lax.optimization_barrier((arrived, sent, first, gates))[0]
     moved = [
@@ -291,30 +291,18 @@
     ]
     other = exchange(arrived)
 
-    def joined(own, after):
-        gate, up, _ = lax.optimization_barrier((w_gate, w_up, after))
-        return call(
-            functools.partial(join_kernel, own),
-            pltpu.VMEM((half, 2 * units), bf),
-            [HBM, HBM],
-            (in_hbm(gate), in_hbm(up)),
-            scratch_shapes=[pltpu.SemaphoreType.DMA((2,))],
-            cost_estimate=None if own else BESIDE,
-        )
-
-    other = exchange(arrived)
     partial = call(
         own_kernel,
-        array((slots, 2 * units), f32),
-        [VMEM] * 2,
-        (arrived.reshape(flat), joined(True, sent)),
+        [array((slots, units), f32)] * 2,
+        [VMEM] * 3,
+        (arrived.reshape(flat), w_gate, w_up),
         cost_estimate=BESIDE,
     )
     hidden = call(
         hidden_kernel,
         array((slots, units)),
-        [VMEM] * 3,
-        (partial, other.reshape(flat), joined(False, partial)),
+        [VMEM] * 5,
+        (*partial, other.reshape(flat), w_gate, w_up),
     )
     all_hidden = lax.all_gather(hidden, "j", axis=0)
     mine, others = call(

time: 106 us -> 107 us (level)
    pallas_call x11 -> x10, Pallas kernels: 11 us -> 11.6 us  [call(): pl.pallas_call(kernel, out_shape=shapes, in_specs=in_specs, out_specs=VME...]
  transfers between devices with their start and end apart: 4 -> 4, of which waited for: 1 -> 2; matrix products, arithmetic and copies ran while one was open for 0% -> 0% of each run, Pallas kernels for 6% -> 5%
where the time goes in v5:
time: 107 us
  blocking collectives  64.4 us (60%)
  starting transfers between devices  21.8 us (20%)
  Pallas kernels  11.6 us (11%)
  waiting for transfers between devices  8.7 us (8%)
    all_to_all x1, blocking collectives, per_device(): lax.all_to_all(spread.reshape(owners, tok_rows // owners, width), ('g', '...  33.8 us
    all_to_all x1, blocking collectives, over_dp(): return lax.all_to_all(x, 'dp', split_axis=0, concat_axis=0, tiled=True)  17.4 us
    all_to_all x1, starting transfers between devices, over_dp(): return lax.all_to_all(x, 'dp', split_axis=0, concat_axis=0, tiled=True)  13.2 us
    pallas_call x10, Pallas kernels, call(): pl.pallas_call(kernel, out_shape=shapes, in_specs=in_specs, out_specs=VME...  11.6 us
    all_gather x1, blocking collectives, per_device(): all_hidden = lax.all_gather(hidden, 'j', axis=0)  11 us
    all_to_all x1, waiting for transfers between devices, over_dp(): return lax.all_to_all(x, 'dp', split_axis=0, concat_axis=0, tiled=True)  7.83 us
    ppermute x2, starting transfers between devices, per_device(): lax.ppermute(block, 'j', [(i, (i + step) % thirds) for i in range(thirds)])  6.74 us
  transfers between devices with their start and end apart: 4, of which 2 were waited for; matrix products, arithmetic and copies ran while one was open for 0% of the time, Pallas kernels for 5%

profile of v5, /device:TPU:8, one launch (start us, length us, event | category | flops | bytes accessed | tf_op | source)
XLA Modules:
  0.0 106.7 jit_solution(14413897262880656611)
XLA Ops:
  0.0 3.0 %shard_map.66 = bf16[512,640]{1,0:T(8,128)(2,1)} custom-call(s32[1,192]{1,0:T(1,128)} %bitcast.20, bf16[192,5120]{1,0:T(8,128)(2,1)} %tokens_ref.1), custom_call_target="tpu_custom_call" | custom-call | tf_op jit(solution)/shard_map/pallas_call | solution.py:216
  3.1 0.0 copy-start
  3.1 13.2 %all-to-all-start = ((bf16[32,16,640]{2,1,0:T(8,128)(2,1)}), bf16[32,16,640]{2,1,0:T(8,128)(2,1)S(1)}, u32[]{:S(2)}, u32[]{:S(2)}) async-start(bf16[32,16,640]{2,1,0:T(8,128)(2,1)} %bitcast.2), calls=%async_computation | async-start | bytes 1310720 | tf_op jit(solution)/shard_map/all_to_all | solution.py:235
  16.2 0.0 copy-done
  16.2 1.3 %shard_map.64 = (bf16[128,1792]{1,0:T(8,128)(2,1)}, bf16[128,1792]{1,0:T(8,128)(2,1)}, bf16[128,1792]{1,0:T(8,128)(2,1)}) custom-call(bf16[128,5120]{1,0:T(8,128)(2,1)S(1)} %copy-done), custom_call_target="tpu_custom_call" | custom-call | tf_op jit(solution)/shard_map/pallas_call | solution.py:216
  17.5 1.9 %collective-permute-start.1 = (bf16[128,1792]{1,0:T(8,128)(2,1)}, bf16[128,1792]{1,0:T(8,128)(2,1)}, u32[]{:S(2)}, u32[]{:S(2)}) collective-permute-start(bf16[128,1792]{1,0:T(8,128)(2,1)} %get-tuple-element.18), channel_id=1, source_target_pairs={{0,2},{2,4},{4,0},{1,3},{3,5},{5,1},{6,8},{8,10},{10,6},{7,9},{9,1... | collective-permute-start | bytes 1376264 | tf_op jit(solution)/shard_map/ppermute | solution.py:289
  19.5 4.8 %collective-permute-start.2 = (bf16[128,1792]{1,0:T(8,128)(2,1)}, bf16[128,1792]{1,0:T(8,128)(2,1)}, u32[]{:S(2)}, u32[]{:S(2)}) collective-permute-start(bf16[128,1792]{1,0:T(8,128)(2,1)} %get-tuple-element.19), channel_id=1, source_target_pairs={{0,4},{2,0},{4,2},{1,5},{3,1},{5,3},{6,10},{8,6},{10,8},{7,11},{9,... | collective-permute-start | bytes 1376264 | tf_op jit(solution)/shard_map/ppermute | solution.py:289
  24.3 0.0 copy-start.3
  24.3 0.0 copy-start.4
  24.3 0.0 copy-start.1
  24.3 1.4 %shard_map.67.up_ref = bf16[5120,128]{1,0:T(8,128)(2,1)S(1)} custom-call(bf16[5120,128]{1,0:T(8,128)(2,1)} %from_ref), custom_call_target="tpu_custom_call" | custom-call | tf_op jit(solution)/shard_map/pallas_call | solution.py:216
  25.8 0.0 copy-done.3
  25.8 0.0 copy-done.4
  25.8 0.2 shard_map.65
  26.0 7.8 %all-to-all-done = bf16[32,16,640]{2,1,0:T(8,128)(2,1)S(1)} async-done(((bf16[32,16,640]{2,1,0:T(8,128)(2,1)}), bf16[32,16,640]{2,1,0:T(8,128)(2,1)S(1)}, u32[]{:S(2)}, u32[]{:S(2)}) %all-to-all-start) | async-done | bytes 655392 | tf_op jit(solution)/shard_map/all_to_all | solution.py:235
  33.9 1.9 %collective-permute-start = (bf16[32,16,640]{2,1,0:T(8,128)(2,1)S(1)}, bf16[32,16,640]{2,1,0:T(8,128)(2,1)S(1)}, u32[]{:S(2)}, u32[]{:S(2)}) collective-permute-start(bf16[32,16,640]{2,1,0:T(8,128)(2,1)S(1)} %all-to-all-done), channel_id=1, source_target_pairs={{0,1},{1,0},{2,3},{3,2},{4,5},{5,4},{6,7},{7,6},{8,9},{9,8},{10,11... | collective-permute-start | bytes 1966088 | tf_op jit(solution)/shard_map/ppermute | solution.py:231
  35.8 0.0 copy-done.1
  35.8 1.2 %shard_map.68 = (f32[128,128]{1,0:T(8,128)S(1)}, f32[128,128]{1,0:T(8,128)S(1)}) custom-call(bf16[512,640]{1,0:T(8,128)(2,1)S(1)} %bitcast.16, bf16[5120,128]{1,0:T(8,128)(2,1)S(1)} %copy-done.1, bf16[5120,128]{1,0:T(8,128)(2,1)S(1)} %shard_map.67.up_ref), custom_call_target="tpu_custom_call" | custom-call | flops 8000000000 | bytes 16777216 | tf_op jit(solution)/shard_map/pallas_call | solution.py:216
  37.0 0.9 collective-permute-done
  37.9 0.0 copy-start.2
  37.9 1.2 %shard_map.69 = bf16[128,128]{1,0:T(8,128)(2,1)S(1)} custom-call(f32[128,128]{1,0:T(8,128)S(1)} %get-tuple-element.26.pre_gate_ref, f32[128,128]{1,0:T(8,128)S(1)} %get-tuple-element.27.pre_up_ref, bf16[512,640]{1,0:T(8,128)(2,1)S(1)} %bitcast.17, bf16[5120,128]{1,0:T(8,128)(2,1)S(1)} %copy-done.1, bf16[5120,128]{1,0:T(8,128)(2,1)S(1)} %shard_map.67.up_ref), custom_call_target="tpu_custom_call" | custom-call | tf_op jit(solution)/shard_map/pallas_call | solution.py:216
  39.1 11.0 %all-gather = bf16[384,128]{1,0:T(8,128)(2,1)S(1)} all-gather(bf16[128,128]{1,0:T(8,128)(2,1)S(1)} %shard_map.69), channel_id=2, replica_groups=mesh['dp'=32,'g'=4,'j'=3,'k'=2] {'j'}, dimensions={0}, use_global_device_ids=true | all-gather | bytes 131072 | tf_op jit(solution)/shard_map/all_gather | solution.py:307
  50.0 0.0 collective-permute-done.1.next_ref
  50.0 0.0 collective-permute-done.2.last_ref
  50.1 0.0 copy-done.2
  50.1 1.7 %shard_map.70 = (f32[128,896]{1,0:T(8,128)S(1)}, bf16[128,896]{1,0:T(8,128)(2,1)S(1)}) custom-call(bf16[3,128,128]{2,1,0:T(8,128)(2,1)S(1)} %bitcast.18, bf16[128,1792]{1,0:T(8,128)(2,1)} %collective-permute-done.1.next_ref, bf16[128,1792]{1,0:T(8,128)(2,1)} %collective-permute-done.2.last_ref, bf16[128,1792]{1,0:T(8,128)(2,1)S(1)} %copy-done.2), custom_call_target="tpu_custom_call" | custom-call | tf_op jit(solution)/shard_map/pallas_call | solution.py:216
  51.7 2.1 %all-gather.1 = bf16[256,896]{1,0:T(8,128)(2,1)S(1)} all-gather(bf16[128,896]{1,0:T(8,128)(2,1)S(1)} %get-tuple-element.30), channel_id=3, replica_groups=mesh['dp'=32,'g'=4,'j'=3,'k'=2] {'k'}, dimensions={0}, use_global_device_ids=true | all-gather | bytes 688128 | tf_op jit(solution)/shard_map/all_gather | solution.py:318
  53.9 0.4 shard_map.71
  54.3 17.4 %all_to_all.15 = bf16[32,16,256]{2,1,0:T(8,128)(2,1)S(1)} all-to-all(bf16[32,16,256]{2,1,0:T(8,128)(2,1)S(1)} %bitcast.14), channel_id=1, replica_groups=mesh['dp'=32,'g'=4,'j'=3,'k'=2] {'dp'}, dimensions={0} | all-to-all | bytes 524288 | tf_op jit(solution)/shard_map/all_to_all | solution.py:235
  71.7 0.4 shard_map.72
  72.1 33.8 %all_to_all.16 = bf16[24,8,896]{2,1,0:T(8,128)(2,1)S(1)} all-to-all(bf16[24,8,896]{2,1,0:T(8,128)(2,1)S(1)} %bitcast.12), channel_id=1, replica_groups=mesh['dp'=32,'g'=4,'j'=3,'k'=2] {'g','j','k'}, dimensions={0} | all-to-all | bytes 688128 | tf_op jit(solution)/shard_map/all_to_all | solution.py:327
  105.9 0.7 shard_map.73
Async XLA Ops:
  3.1 13.2 %copy-start = (bf16[128,5120]{1,0:T(8,128)(2,1)S(1)}, bf16[128,5120]{1,0:T(8,128)(2,1)}, u32[]{:S(2)}) copy-start(bf16[128,5120]{1,0:T(8,128)(2,1)} %down_ref.1) | copy-start | bytes 3932164
  3.1 30.8 %all-to-all-start = ((bf16[32,16,640]{2,1,0:T(8,128)(2,1)}), bf16[32,16,640]{2,1,0:T(8,128)(2,1)S(1)}, u32[]{:S(2)}, u32[]{:S(2)}) async-start(bf16[32,16,640]{2,1,0:T(8,128)(2,1)} %bitcast.2), calls=%async_computation | async-start | bytes 1310720 | tf_op jit(solution)/shard_map/all_to_all | solution.py:235
  17.5 32.5 %collective-permute-start.1 = (bf16[128,1792]{1,0:T(8,128)(2,1)}, bf16[128,1792]{1,0:T(8,128)(2,1)}, u32[]{:S(2)}, u32[]{:S(2)}) collective-permute-start(bf16[128,1792]{1,0:T(8,128)(2,1)} %get-tuple-element.18), channel_id=1, source_target_pairs={{0,2},{2,4},{4,0},{1,3},{3,5},{5,1},{6,8},{8,10},{10,6},{7,9},{9,1... | collective-permute-start | bytes 1376264 | tf_op jit(solution)/shard_map/ppermute | solution.py:289
  19.5 30.6 %collective-permute-start.2 = (bf16[128,1792]{1,0:T(8,128)(2,1)}, bf16[128,1792]{1,0:T(8,128)(2,1)}, u32[]{:S(2)}, u32[]{:S(2)}) collective-permute-start(bf16[128,1792]{1,0:T(8,128)(2,1)} %get-tuple-element.19), channel_id=1, source_target_pairs={{0,4},{2,0},{4,2},{1,5},{3,1},{5,3},{6,10},{8,6},{10,8},{7,11},{9,... | collective-permute-start | bytes 1376264 | tf_op jit(solution)/shard_map/ppermute | solution.py:289
  24.3 1.5 %copy-start.3 = (f32[192,8]{0,1:T(8,128)S(1)}, f32[192,8]{0,1:T(8,128)}, u32[]{:S(2)}) copy-start(f32[192,8]{0,1:T(8,128)} %param.7) | copy-start | bytes 18436
  24.3 1.5 %copy-start.4 = (s32[192,1]{0,1:T(1,128)S(1)}, s32[192,1]{0,1:T(1,128)}, u32[]{:S(2)}) copy-start(s32[192,1]{0,1:T(1,128)} %param.8) | copy-start | bytes 2308
  24.3 11.5 %copy-start.1 = (bf16[5120,128]{1,0:T(8,128)(2,1)S(1)}, bf16[5120,128]{1,0:T(8,128)(2,1)}, u32[]{:S(2)}) copy-start(bf16[5120,128]{1,0:T(8,128)(2,1)} %gate_ref.3) | copy-start | bytes 3932164
  33.9 4.0 %collective-permute-start = (bf16[32,16,640]{2,1,0:T(8,128)(2,1)S(1)}, bf16[32,16,640]{2,1,0:T(8,128)(2,1)S(1)}, u32[]{:S(2)}, u32[]{:S(2)}) collective-permute-start(bf16[32,16,640]{2,1,0:T(8,128)(2,1)S(1)} %all-to-all-done), channel_id=1, source_target_pairs={{0,1},{1,0},{2,3},{3,2},{4,5},{5,4},{6,7},{7,6},{8,9},{9,8},{10,11... | collective-permute-start | bytes 1966088 | tf_op jit(solution)/shard_map/ppermute | solution.py:231
  37.9 12.2 %copy-start.2 = (bf16[128,1792]{1,0:T(8,128)(2,1)S(1)}, bf16[128,1792]{1,0:T(8,128)(2,1)}, u32[]{:S(2)}) copy-start(bf16[128,1792]{1,0:T(8,128)(2,1)} %get-tuple-element.28.kept_ref) | copy-start | bytes 1376260
